TPU v7x, 128 devices: a whole 4x4x4 slice. The times are simulated.
128 devices in a mesh: region: 32 (over y, x, z_lo), view: 4 (over z_hi, core).
Axes of the slice: x: 4, y: 4, z: 4 (z_hi: 2, z_lo: 2; z = z_hi * 2 + z_lo), core: 2. Of those that a mesh axis runs over, the one named last changes fastest.
Arguments:
- embeddings: bfloat16 [32768, 768], P(('region', 'view')), may hold values from -6 to 6
- region_ids: int32 [32768], P(('region', 'view')), may hold values from 0 to 16383, as said below
- tile_ids: int32 [32768], P(('region', 'view')), may hold values from 0 to 2047, as said below
- logit_scale: float32 [1], replicated, may hold values from 1.5 to 3
- logit_bias: float32 [1], replicated, may hold values from -7 to -5
Outputs:
- grads: float32 [32768, 768], P(('region', 'view'))
Inputs may be any that keep to these rules, and one draw needn't show every extreme that they name: `region_ids`: every region id appears exactly twice, once for each view. `tile_ids`: embeddings with the same region id have the same tile id; every tile holds exactly 8 regions.
All inputs are finite; a program needn't handle non-finite values.
Results may differ from a plain program's by a relative error of at most 0.00075.
Values may be sent and summed in bfloat16 or wider, within the bound.
A program may use at most 64 MiB of HBM per device.

v0:
```python
import math

import jax
import jax.numpy as jnp
from jax import lax
from jax.sharding import PartitionSpec as P

D = 768


def shifted(value, axis, steps):
    count = lax.axis_size(axis)
    pairs = [(source, (source + steps) % count) for source in range(count)]
    return lax.ppermute(value, axis, pairs)


def slope_block(
    queries,
    query_ids,
    query_tiles,
    query_first,
    keys,
    key_ids,
    key_tiles,
    key_first,
    scale,
    bias,
    weight,
):
    logits = (
        jnp.einsum("qd,kd->qk", queries, keys, preferred_element_type=jnp.float32) * scale + bias
    )
    query_index = query_first + jnp.arange(queries.shape[0], dtype=jnp.int32)
    key_index = key_first + jnp.arange(keys.shape[0], dtype=jnp.int32)
    same = query_ids[:, None] == key_ids[None, :]
    sign = jnp.where(same, 1.0, -1.0).astype(jnp.float32)
    keep = (query_index[:, None] != key_index[None, :]) & (
        same | (query_tiles[:, None] != key_tiles[None, :])
    )
    slope = jnp.where(keep, -sign * jax.nn.sigmoid(-sign * logits), 0.0)
    return (slope * weight).astype(jnp.bfloat16)


def local(embeddings, region_ids, tile_ids, logit_scale, logit_bias):
    rows = embeddings.shape[0]
    regions_count = lax.axis_size("region")
    views_count = lax.axis_size("view")
    place = lax.axis_index("region")
    lane = lax.axis_index("view")
    scale = logit_scale[0] * (1.0 / math.sqrt(D))
    bias = logit_bias[0]
    queries, query_ids, query_tiles = (
        lax.all_gather(embeddings, "view", axis=0, tiled=True),
        lax.all_gather(region_ids, "view", axis=0, tiled=True),
        lax.all_gather(tile_ids, "view", axis=0, tiled=True),
    )
    query_first = place * views_count * rows

    def anchor(step):
        return ((place - step) % regions_count * views_count + lane) * rows

    def slopes(keys, key_ids, key_tiles, step, weight):
        return slope_block(
            queries,
            query_ids,
            query_tiles,
            query_first,
            keys,
            key_ids,
            key_tiles,
            anchor(step),
            scale,
            bias,
            weight,
        )

    one = jnp.float32(1.0)
    half = regions_count // 2
    first = slopes(embeddings, region_ids, tile_ids, 0, one)
    query_grad = jnp.dot(first, embeddings, preferred_element_type=jnp.float32)
    key_grad = jnp.einsum("qk,qd->kd", first, queries, preferred_element_type=jnp.float32)

    def advance(step, state):
        keys, key_ids, key_tiles, carried, gathered_grad = state
        keys, key_ids, key_tiles = shifted((keys, key_ids, key_tiles), "region", 1)
        carried = shifted(carried, "region", 1)
        weight = jnp.where(step == half, 1.0, 2.0).astype(jnp.float32)
        slope = slopes(keys, key_ids, key_tiles, step, weight)
        gathered_grad = gathered_grad + jnp.dot(slope, keys, preferred_element_type=jnp.float32)
        carried = carried + jnp.einsum(
            "qk,qd->kd", slope, queries, preferred_element_type=jnp.float32
        )
        return (keys, key_ids, key_tiles, carried, gathered_grad)

    state = lax.fori_loop(
        1, half + 1, advance, (embeddings, region_ids, tile_ids, key_grad, query_grad)
    )
    extra = shifted(state[3], "region", -half)
    gathered = state[4]
    owned = lax.psum_scatter(gathered, "view", scatter_dimension=0, tiled=True)
    return (owned + extra) * scale


def solution(mesh):
    placed = (P(("region", "view"), None), P(("region", "view")), P(("region", "view")), P(), P())
    return jax.shard_map(
        local, mesh=mesh, in_specs=placed, out_specs=P(("region", "view"), None), check_vma=False
    )
```

profile of v0, /device:TPU:1, one launch (start us, length us, event | category | flops | bytes accessed | tf_op | source)
XLA Modules:
  0.0 568.8 jit_solution(10244508222193856289)
XLA Ops:
  12.2 8.5 %all-gather.1 = s32[4,1,256]{2,1,0:T(1,128)S(1)} all-gather(s32[1,1,256]{2,1,0:T(1,128)} %bitcast.2), channel_id=1, replica_groups=mesh['region'=32,'view'=4] {'view'}, dimensions={0}, use_global_device_ids=true | all-gather | bytes 5120 | tf_op jit(solution)/shard_map/all_gather | solution.py:55
  20.7 7.0 %all-gather = s32[4,1,256]{2,1,0:T(1,128)S(1)} all-gather(s32[1,1,256]{2,1,0:T(1,128)} %bitcast), channel_id=1, replica_groups=mesh['region'=32,'view'=4] {'view'}, dimensions={0}, use_global_device_ids=true | all-gather | bytes 5120 | tf_op jit(solution)/shard_map/all_gather | solution.py:54
  27.7 10.7 %all-gather.4.cloned.1.call-done = bf16[1024,768]{1,0:T(8,128)(2,1)} async-done(((bf16[256,768]{1,0:T(8,128)(2,1)}), bf16[1024,768]{1,0:T(8,128)(2,1)}) %all-gather.4.cloned.1.call-update) | async-done | bytes 1572880 | tf_op jit(solution)/shard_map/all_gather | solution.py:53
  43.9 453.7 %while.23 = (s32[]{:T(128)}, bf16[256,768]{1,0:T(8,128)(2,1)}, s32[256]{0:T(256)}, s32[256]{0:T(256)}, f32[256,768]{1,0:T(8,128)}, /*index=5*/f32[1024,768]{1,0:...) while((s32[]{:T(128)}, bf16[256,768]{1,0:T(8,128)(2,1)}, ...), condition=%wide.region_1.2_spmd, body=%wide.region_0.1_spmd.sunk | while | flops 1213400320 | bytes 25199184 | solution.py:95
  49.2 9.6 %collective-permute-done.2 = s32[256]{0:T(256)S(1)} collective-permute-done((s32[256]{0:T(256)}, s32[256]{0:T(256)S(1)}, u32[]{:S(2)}, u32[]{:S(2)}) %collective-permute-start.2) | collective-permute-done | bytes 1056 | tf_op jit(solution)/shard_map/while/body/eval_jaxpr/ppermute | solution.py:14
  64.3 11.5 %collective-permute-done.3 = f32[256,768]{1,0:T(8,128)} collective-permute-done((f32[256,768]{1,0:T(8,128)}, f32[256,768]{1,0:T(8,128)}, u32[]{:S(2)}, u32[]{:S(2)}) %collective-permute-start.3) | collective-permute-done | bytes 786464 | tf_op jit(solution)/shard_map/while/body/eval_jaxpr/ppermute | solution.py:14
  80.4 12.0 %collective-permute-done.2 = s32[256]{0:T(256)S(1)} collective-permute-done((s32[256]{0:T(256)}, s32[256]{0:T(256)S(1)}, u32[]{:S(2)}, u32[]{:S(2)}) %collective-permute-start.2) | collective-permute-done | bytes 1056 | tf_op jit(solution)/shard_map/while/body/eval_jaxpr/ppermute | solution.py:14
  97.9 11.5 %collective-permute-done.3 = f32[256,768]{1,0:T(8,128)} collective-permute-done((f32[256,768]{1,0:T(8,128)}, f32[256,768]{1,0:T(8,128)}, u32[]{:S(2)}, u32[]{:S(2)}) %collective-permute-start.3) | collective-permute-done | bytes 786464 | tf_op jit(solution)/shard_map/while/body/eval_jaxpr/ppermute | solution.py:14
  112.7 12.3 %collective-permute-done.2 = s32[256]{0:T(256)S(1)} collective-permute-done((s32[256]{0:T(256)}, s32[256]{0:T(256)S(1)}, u32[]{:S(2)}, u32[]{:S(2)}) %collective-permute-start.2) | collective-permute-done | bytes 1056 | tf_op jit(solution)/shard_map/while/body/eval_jaxpr/ppermute | solution.py:14
  130.5 11.5 %collective-permute-done.3 = f32[256,768]{1,0:T(8,128)} collective-permute-done((f32[256,768]{1,0:T(8,128)}, f32[256,768]{1,0:T(8,128)}, u32[]{:S(2)}, u32[]{:S(2)}) %collective-permute-start.3) | collective-permute-done | bytes 786464 | tf_op jit(solution)/shard_map/while/body/eval_jaxpr/ppermute | solution.py:14
  145.3 11.4 %collective-permute-done.2 = s32[256]{0:T(256)S(1)} collective-permute-done((s32[256]{0:T(256)}, s32[256]{0:T(256)S(1)}, u32[]{:S(2)}, u32[]{:S(2)}) %collective-permute-start.2) | collective-permute-done | bytes 1056 | tf_op jit(solution)/shard_map/while/body/eval_jaxpr/ppermute | solution.py:14
  162.3 11.5 %collective-permute-done.3 = f32[256,768]{1,0:T(8,128)} collective-permute-done((f32[256,768]{1,0:T(8,128)}, f32[256,768]{1,0:T(8,128)}, u32[]{:S(2)}, u32[]{:S(2)}) %collective-permute-start.3) | collective-permute-done | bytes 786464 | tf_op jit(solution)/shard_map/while/body/eval_jaxpr/ppermute | solution.py:14
  177.1 10.4 %collective-permute-done.2 = s32[256]{0:T(256)S(1)} collective-permute-done((s32[256]{0:T(256)}, s32[256]{0:T(256)S(1)}, u32[]{:S(2)}, u32[]{:S(2)}) %collective-permute-start.2) | collective-permute-done | bytes 1056 | tf_op jit(solution)/shard_map/while/body/eval_jaxpr/ppermute | solution.py:14
  193.0 11.6 %collective-permute-done.3 = f32[256,768]{1,0:T(8,128)} collective-permute-done((f32[256,768]{1,0:T(8,128)}, f32[256,768]{1,0:T(8,128)}, u32[]{:S(2)}, u32[]{:S(2)}) %collective-permute-start.3) | collective-permute-done | bytes 786464 | tf_op jit(solution)/shard_map/while/body/eval_jaxpr/ppermute | solution.py:14
  207.9 10.4 %collective-permute-done.2 = s32[256]{0:T(256)S(1)} collective-permute-done((s32[256]{0:T(256)}, s32[256]{0:T(256)S(1)}, u32[]{:S(2)}, u32[]{:S(2)}) %collective-permute-start.2) | collective-permute-done | bytes 1056 | tf_op jit(solution)/shard_map/while/body/eval_jaxpr/ppermute | solution.py:14
  223.8 10.6 %collective-permute-done.3 = f32[256,768]{1,0:T(8,128)} collective-permute-done((f32[256,768]{1,0:T(8,128)}, f32[256,768]{1,0:T(8,128)}, u32[]{:S(2)}, u32[]{:S(2)}) %collective-permute-start.3) | collective-permute-done | bytes 786464 | tf_op jit(solution)/shard_map/while/body/eval_jaxpr/ppermute | solution.py:14
  237.8 10.4 %collective-permute-done.2 = s32[256]{0:T(256)S(1)} collective-permute-done((s32[256]{0:T(256)}, s32[256]{0:T(256)S(1)}, u32[]{:S(2)}, u32[]{:S(2)}) %collective-permute-start.2) | collective-permute-done | bytes 1056 | tf_op jit(solution)/shard_map/while/body/eval_jaxpr/ppermute | solution.py:14
  253.7 9.7 %collective-permute-done.3 = f32[256,768]{1,0:T(8,128)} collective-permute-done((f32[256,768]{1,0:T(8,128)}, f32[256,768]{1,0:T(8,128)}, u32[]{:S(2)}, u32[]{:S(2)}) %collective-permute-start.3) | collective-permute-done | bytes 786464 | tf_op jit(solution)/shard_map/while/body/eval_jaxpr/ppermute | solution.py:14
  266.8 10.4 %collective-permute-done.2 = s32[256]{0:T(256)S(1)} collective-permute-done((s32[256]{0:T(256)}, s32[256]{0:T(256)S(1)}, u32[]{:S(2)}, u32[]{:S(2)}) %collective-permute-start.2) | collective-permute-done | bytes 1056 | tf_op jit(solution)/shard_map/while/body/eval_jaxpr/ppermute | solution.py:14
  282.7 8.8 %collective-permute-done.3 = f32[256,768]{1,0:T(8,128)} collective-permute-done((f32[256,768]{1,0:T(8,128)}, f32[256,768]{1,0:T(8,128)}, u32[]{:S(2)}, u32[]{:S(2)}) %collective-permute-start.3) | collective-permute-done | bytes 786464 | tf_op jit(solution)/shard_map/while/body/eval_jaxpr/ppermute | solution.py:14
  294.8 10.4 %collective-permute-done.2 = s32[256]{0:T(256)S(1)} collective-permute-done((s32[256]{0:T(256)}, s32[256]{0:T(256)S(1)}, u32[]{:S(2)}, u32[]{:S(2)}) %collective-permute-start.2) | collective-permute-done | bytes 1056 | tf_op jit(solution)/shard_map/while/body/eval_jaxpr/ppermute | solution.py:14
  310.7 7.9 %collective-permute-done.3 = f32[256,768]{1,0:T(8,128)} collective-permute-done((f32[256,768]{1,0:T(8,128)}, f32[256,768]{1,0:T(8,128)}, u32[]{:S(2)}, u32[]{:S(2)}) %collective-permute-start.3) | collective-permute-done | bytes 786464 | tf_op jit(solution)/shard_map/while/body/eval_jaxpr/ppermute | solution.py:14
  321.9 10.4 %collective-permute-done.2 = s32[256]{0:T(256)S(1)} collective-permute-done((s32[256]{0:T(256)}, s32[256]{0:T(256)S(1)}, u32[]{:S(2)}, u32[]{:S(2)}) %collective-permute-start.2) | collective-permute-done | bytes 1056 | tf_op jit(solution)/shard_map/while/body/eval_jaxpr/ppermute | solution.py:14
  337.9 6.8 %collective-permute-done.3 = f32[256,768]{1,0:T(8,128)} collective-permute-done((f32[256,768]{1,0:T(8,128)}, f32[256,768]{1,0:T(8,128)}, u32[]{:S(2)}, u32[]{:S(2)}) %collective-permute-start.3) | collective-permute-done | bytes 786464 | tf_op jit(solution)/shard_map/while/body/eval_jaxpr/ppermute | solution.py:14
  348.0 10.4 %collective-permute-done.2 = s32[256]{0:T(256)S(1)} collective-permute-done((s32[256]{0:T(256)}, s32[256]{0:T(256)S(1)}, u32[]{:S(2)}, u32[]{:S(2)}) %collective-permute-start.2) | collective-permute-done | bytes 1056 | tf_op jit(solution)/shard_map/while/body/eval_jaxpr/ppermute | solution.py:14
  373.1 10.6 %collective-permute-done.2 = s32[256]{0:T(256)S(1)} collective-permute-done((s32[256]{0:T(256)}, s32[256]{0:T(256)S(1)}, u32[]{:S(2)}, u32[]{:S(2)}) %collective-permute-start.2) | collective-permute-done | bytes 1056 | tf_op jit(solution)/shard_map/while/body/eval_jaxpr/ppermute | solution.py:14
  397.5 11.6 %collective-permute-done.2 = s32[256]{0:T(256)S(1)} collective-permute-done((s32[256]{0:T(256)}, s32[256]{0:T(256)S(1)}, u32[]{:S(2)}, u32[]{:S(2)}) %collective-permute-start.2) | collective-permute-done | bytes 1056 | tf_op jit(solution)/shard_map/while/body/eval_jaxpr/ppermute | solution.py:14
  421.8 12.6 %collective-permute-done.2 = s32[256]{0:T(256)S(1)} collective-permute-done((s32[256]{0:T(256)}, s32[256]{0:T(256)S(1)}, u32[]{:S(2)}, u32[]{:S(2)}) %collective-permute-start.2) | collective-permute-done | bytes 1056 | tf_op jit(solution)/shard_map/while/body/eval_jaxpr/ppermute | solution.py:14
  446.2 13.6 %collective-permute-done.2 = s32[256]{0:T(256)S(1)} collective-permute-done((s32[256]{0:T(256)}, s32[256]{0:T(256)S(1)}, u32[]{:S(2)}, u32[]{:S(2)}) %collective-permute-start.2) | collective-permute-done | bytes 1056 | tf_op jit(solution)/shard_map/while/body/eval_jaxpr/ppermute | solution.py:14
  471.7 15.0 %collective-permute-done.2 = s32[256]{0:T(256)S(1)} collective-permute-done((s32[256]{0:T(256)}, s32[256]{0:T(256)S(1)}, u32[]{:S(2)}, u32[]{:S(2)}) %collective-permute-start.2) | collective-permute-done | bytes 1056 | tf_op jit(solution)/shard_map/while/body/eval_jaxpr/ppermute | solution.py:14
  505.4 9.6 %collective-permute-done.4 = f32[256,768]{1,0:T(8,128)S(1)} collective-permute-done((f32[256,768]{1,0:T(8,128)}, f32[256,768]{1,0:T(8,128)S(1)}, u32[]{:S(2)}, u32[]{:S(2)}) %collective-permute-start.4) | collective-permute-done | bytes 786464 | tf_op jit(solution)/shard_map/ppermute | solution.py:14
  515.0 44.9 %reduce-scatter.2.cloned.1.call-done = f32[256,768]{1,0:T(8,128)} async-done(((f32[1024,768]{1,0:T(8,128)}), f32[256,768]{1,0:T(8,128)}) %reduce-scatter.2.cloned.1.call-update) | async-done | bytes 786448 | tf_op jit(solution)/shard_map/reduce_scatter | solution.py:100
  (284 shorter events, 189.6 us)
Async XLA Ops:
  6.5 31.9 %all-gather.4.cloned.1.call-start = ((), (), s32[]{:S(2)}) async-start(), calls=%async_computation.1 | async-start | bytes 1966080 | tf_op jit(solution)/shard_map/all_gather | solution.py:53
  10.8 549.1 %reduce-scatter.2.cloned.1.call-start = ((), (), s32[]{:S(2)}) async-start(), calls=%async_computation.2 | async-start | bytes 3932160 | tf_op jit(solution)/shard_map/reduce_scatter | solution.py:100
  43.9 16.0 %collective-permute-start = (bf16[256,768]{1,0:T(8,128)(2,1)}, bf16[256,768]{1,0:T(8,128)(2,1)S(1)}, u32[]{:S(2)}, u32[]{:S(2)}) collective-permute-start(bf16[256,768]{1,0:T(8,128)(2,1)} %get-tuple-element.476), channel_id=1, source_target_pairs={{0,4},{4,8},{8,12},{12,16},{16,20},{20,24},{24,28},{28,32},{32,36}... | collective-permute-start | bytes 1179656 | tf_op jit(solution)/shard_map/while/body/eval_jaxpr/ppermute | solution.py:14
  44.2 14.5 %collective-permute-start.2 = (s32[256]{0:T(256)}, s32[256]{0:T(256)S(1)}, u32[]{:S(2)}, u32[]{:S(2)}) collective-permute-start(s32[256]{0:T(256)} %get-tuple-element.478), channel_id=1, source_target_pairs={{0,4},{4,8},{8,12},{12,16},{16,20},{20,24},{24,28},{28,32},{32,36}... | collective-permute-start | bytes 3080 | tf_op jit(solution)/shard_map/while/body/eval_jaxpr/ppermute | solution.py:14
  46.6 29.1 %collective-permute-start.3 = (f32[256,768]{1,0:T(8,128)}, f32[256,768]{1,0:T(8,128)}, u32[]{:S(2)}, u32[]{:S(2)}) collective-permute-start(f32[256,768]{1,0:T(8,128)} %get-tuple-element.479), channel_id=1, source_target_pairs={{0,4},{4,8},{8,12},{12,16},{16,20},{20,24},{24,28},{28,32},{32,36}... | collective-permute-start | bytes 2359304 | tf_op jit(solution)/shard_map/while/body/eval_jaxpr/ppermute | solution.py:14
  78.4 15.1 %collective-permute-start = (bf16[256,768]{1,0:T(8,128)(2,1)}, bf16[256,768]{1,0:T(8,128)(2,1)S(1)}, u32[]{:S(2)}, u32[]{:S(2)}) collective-permute-start(bf16[256,768]{1,0:T(8,128)(2,1)} %get-tuple-element.476), channel_id=1, source_target_pairs={{0,4},{4,8},{8,12},{12,16},{16,20},{20,24},{24,28},{28,32},{32,36}... | collective-permute-start | bytes 1179656 | tf_op jit(solution)/shard_map/while/body/eval_jaxpr/ppermute | solution.py:14
  78.4 14.0 %collective-permute-start.2 = (s32[256]{0:T(256)}, s32[256]{0:T(256)S(1)}, u32[]{:S(2)}, u32[]{:S(2)}) collective-permute-start(s32[256]{0:T(256)} %get-tuple-element.478), channel_id=1, source_target_pairs={{0,4},{4,8},{8,12},{12,16},{16,20},{20,24},{24,28},{28,32},{32,36}... | collective-permute-start | bytes 3080 | tf_op jit(solution)/shard_map/while/body/eval_jaxpr/ppermute | solution.py:14
  78.4 14.5 %collective-permute-start.1 = (s32[256]{0:T(256)}, s32[256]{0:T(256)S(1)}, u32[]{:S(2)}, u32[]{:S(2)}) collective-permute-start(s32[256]{0:T(256)} %get-tuple-element.477), channel_id=1, source_target_pairs={{0,4},{4,8},{8,12},{12,16},{16,20},{20,24},{24,28},{28,32},{32,36}... | collective-permute-start | bytes 3080 | tf_op jit(solution)/shard_map/while/body/eval_jaxpr/ppermute | solution.py:14
  78.4 30.9 %collective-permute-start.3 = (f32[256,768]{1,0:T(8,128)}, f32[256,768]{1,0:T(8,128)}, u32[]{:S(2)}, u32[]{:S(2)}) collective-permute-start(f32[256,768]{1,0:T(8,128)} %get-tuple-element.479), channel_id=1, source_target_pairs={{0,4},{4,8},{8,12},{12,16},{16,20},{20,24},{24,28},{28,32},{32,36}... | collective-permute-start | bytes 2359304 | tf_op jit(solution)/shard_map/while/body/eval_jaxpr/ppermute | solution.py:14
  112.0 14.2 %collective-permute-start = (bf16[256,768]{1,0:T(8,128)(2,1)}, bf16[256,768]{1,0:T(8,128)(2,1)S(1)}, u32[]{:S(2)}, u32[]{:S(2)}) collective-permute-start(bf16[256,768]{1,0:T(8,128)(2,1)} %get-tuple-element.476), channel_id=1, source_target_pairs={{0,4},{4,8},{8,12},{12,16},{16,20},{20,24},{24,28},{28,32},{32,36}... | collective-permute-start | bytes 1179656 | tf_op jit(solution)/shard_map/while/body/eval_jaxpr/ppermute | solution.py:14
  112.0 30.0 %collective-permute-start.3 = (f32[256,768]{1,0:T(8,128)}, f32[256,768]{1,0:T(8,128)}, u32[]{:S(2)}, u32[]{:S(2)}) collective-permute-start(f32[256,768]{1,0:T(8,128)} %get-tuple-element.479), channel_id=1, source_target_pairs={{0,4},{4,8},{8,12},{12,16},{16,20},{20,24},{24,28},{28,32},{32,36}... | collective-permute-start | bytes 2359304 | tf_op jit(solution)/shard_map/while/body/eval_jaxpr/ppermute | solution.py:14
  144.6 29.1 %collective-permute-start.3 = (f32[256,768]{1,0:T(8,128)}, f32[256,768]{1,0:T(8,128)}, u32[]{:S(2)}, u32[]{:S(2)}) collective-permute-start(f32[256,768]{1,0:T(8,128)} %get-tuple-element.479), channel_id=1, source_target_pairs={{0,4},{4,8},{8,12},{12,16},{16,20},{20,24},{24,28},{28,32},{32,36}... | collective-permute-start | bytes 2359304 | tf_op jit(solution)/shard_map/while/body/eval_jaxpr/ppermute | solution.py:14
  176.4 28.2 %collective-permute-start.3 = (f32[256,768]{1,0:T(8,128)}, f32[256,768]{1,0:T(8,128)}, u32[]{:S(2)}, u32[]{:S(2)}) collective-permute-start(f32[256,768]{1,0:T(8,128)} %get-tuple-element.479), channel_id=1, source_target_pairs={{0,4},{4,8},{8,12},{12,16},{16,20},{20,24},{24,28},{28,32},{32,36}... | collective-permute-start | bytes 2359304 | tf_op jit(solution)/shard_map/while/body/eval_jaxpr/ppermute | solution.py:14
  207.2 27.3 %collective-permute-start.3 = (f32[256,768]{1,0:T(8,128)}, f32[256,768]{1,0:T(8,128)}, u32[]{:S(2)}, u32[]{:S(2)}) collective-permute-start(f32[256,768]{1,0:T(8,128)} %get-tuple-element.479), channel_id=1, source_target_pairs={{0,4},{4,8},{8,12},{12,16},{16,20},{20,24},{24,28},{28,32},{32,36}... | collective-permute-start | bytes 2359304 | tf_op jit(solution)/shard_map/while/body/eval_jaxpr/ppermute | solution.py:14
  237.1 26.3 %collective-permute-start.3 = (f32[256,768]{1,0:T(8,128)}, f32[256,768]{1,0:T(8,128)}, u32[]{:S(2)}, u32[]{:S(2)}) collective-permute-start(f32[256,768]{1,0:T(8,128)} %get-tuple-element.479), channel_id=1, source_target_pairs={{0,4},{4,8},{8,12},{12,16},{16,20},{20,24},{24,28},{28,32},{32,36}... | collective-permute-start | bytes 2359304 | tf_op jit(solution)/shard_map/while/body/eval_jaxpr/ppermute | solution.py:14
  266.1 25.4 %collective-permute-start.3 = (f32[256,768]{1,0:T(8,128)}, f32[256,768]{1,0:T(8,128)}, u32[]{:S(2)}, u32[]{:S(2)}) collective-permute-start(f32[256,768]{1,0:T(8,128)} %get-tuple-element.479), channel_id=1, source_target_pairs={{0,4},{4,8},{8,12},{12,16},{16,20},{20,24},{24,28},{28,32},{32,36}... | collective-permute-start | bytes 2359304 | tf_op jit(solution)/shard_map/while/body/eval_jaxpr/ppermute | solution.py:14
  294.1 24.5 %collective-permute-start.3 = (f32[256,768]{1,0:T(8,128)}, f32[256,768]{1,0:T(8,128)}, u32[]{:S(2)}, u32[]{:S(2)}) collective-permute-start(f32[256,768]{1,0:T(8,128)} %get-tuple-element.479), channel_id=1, source_target_pairs={{0,4},{4,8},{8,12},{12,16},{16,20},{20,24},{24,28},{28,32},{32,36}... | collective-permute-start | bytes 2359304 | tf_op jit(solution)/shard_map/while/body/eval_jaxpr/ppermute | solution.py:14
  321.2 23.5 %collective-permute-start.3 = (f32[256,768]{1,0:T(8,128)}, f32[256,768]{1,0:T(8,128)}, u32[]{:S(2)}, u32[]{:S(2)}) collective-permute-start(f32[256,768]{1,0:T(8,128)} %get-tuple-element.479), channel_id=1, source_target_pairs={{0,4},{4,8},{8,12},{12,16},{16,20},{20,24},{24,28},{28,32},{32,36}... | collective-permute-start | bytes 2359304 | tf_op jit(solution)/shard_map/while/body/eval_jaxpr/ppermute | solution.py:14
  347.3 22.4 %collective-permute-start.3 = (f32[256,768]{1,0:T(8,128)}, f32[256,768]{1,0:T(8,128)}, u32[]{:S(2)}, u32[]{:S(2)}) collective-permute-start(f32[256,768]{1,0:T(8,128)} %get-tuple-element.479), channel_id=1, source_target_pairs={{0,4},{4,8},{8,12},{12,16},{16,20},{20,24},{24,28},{28,32},{32,36}... | collective-permute-start | bytes 2359304 | tf_op jit(solution)/shard_map/while/body/eval_jaxpr/ppermute | solution.py:14
  372.4 21.7 %collective-permute-start.3 = (f32[256,768]{1,0:T(8,128)}, f32[256,768]{1,0:T(8,128)}, u32[]{:S(2)}, u32[]{:S(2)}) collective-permute-start(f32[256,768]{1,0:T(8,128)} %get-tuple-element.479), channel_id=1, source_target_pairs={{0,4},{4,8},{8,12},{12,16},{16,20},{20,24},{24,28},{28,32},{32,36}... | collective-permute-start | bytes 2359304 | tf_op jit(solution)/shard_map/while/body/eval_jaxpr/ppermute | solution.py:14
  396.8 21.7 %collective-permute-start.3 = (f32[256,768]{1,0:T(8,128)}, f32[256,768]{1,0:T(8,128)}, u32[]{:S(2)}, u32[]{:S(2)}) collective-permute-start(f32[256,768]{1,0:T(8,128)} %get-tuple-element.479), channel_id=1, source_target_pairs={{0,4},{4,8},{8,12},{12,16},{16,20},{20,24},{24,28},{28,32},{32,36}... | collective-permute-start | bytes 2359304 | tf_op jit(solution)/shard_map/while/body/eval_jaxpr/ppermute | solution.py:14
  421.1 14.4 %collective-permute-start = (bf16[256,768]{1,0:T(8,128)(2,1)}, bf16[256,768]{1,0:T(8,128)(2,1)S(1)}, u32[]{:S(2)}, u32[]{:S(2)}) collective-permute-start(bf16[256,768]{1,0:T(8,128)(2,1)} %get-tuple-element.476), channel_id=1, source_target_pairs={{0,4},{4,8},{8,12},{12,16},{16,20},{20,24},{24,28},{28,32},{32,36}... | collective-permute-start | bytes 1179656 | tf_op jit(solution)/shard_map/while/body/eval_jaxpr/ppermute | solution.py:14
  421.1 21.8 %collective-permute-start.3 = (f32[256,768]{1,0:T(8,128)}, f32[256,768]{1,0:T(8,128)}, u32[]{:S(2)}, u32[]{:S(2)}) collective-permute-start(f32[256,768]{1,0:T(8,128)} %get-tuple-element.479), channel_id=1, source_target_pairs={{0,4},{4,8},{8,12},{12,16},{16,20},{20,24},{24,28},{28,32},{32,36}... | collective-permute-start | bytes 2359304 | tf_op jit(solution)/shard_map/while/body/eval_jaxpr/ppermute | solution.py:14
  445.5 15.5 %collective-permute-start = (bf16[256,768]{1,0:T(8,128)(2,1)}, bf16[256,768]{1,0:T(8,128)(2,1)S(1)}, u32[]{:S(2)}, u32[]{:S(2)}) collective-permute-start(bf16[256,768]{1,0:T(8,128)(2,1)} %get-tuple-element.476), channel_id=1, source_target_pairs={{0,4},{4,8},{8,12},{12,16},{16,20},{20,24},{24,28},{28,32},{32,36}... | collective-permute-start | bytes 1179656 | tf_op jit(solution)/shard_map/while/body/eval_jaxpr/ppermute | solution.py:14
  445.5 14.3 %collective-permute-start.2 = (s32[256]{0:T(256)}, s32[256]{0:T(256)S(1)}, u32[]{:S(2)}, u32[]{:S(2)}) collective-permute-start(s32[256]{0:T(256)} %get-tuple-element.478), channel_id=1, source_target_pairs={{0,4},{4,8},{8,12},{12,16},{16,20},{20,24},{24,28},{28,32},{32,36}... | collective-permute-start | bytes 3080 | tf_op jit(solution)/shard_map/while/body/eval_jaxpr/ppermute | solution.py:14
  445.5 14.9 %collective-permute-start.1 = (s32[256]{0:T(256)}, s32[256]{0:T(256)S(1)}, u32[]{:S(2)}, u32[]{:S(2)}) collective-permute-start(s32[256]{0:T(256)} %get-tuple-element.477), channel_id=1, source_target_pairs={{0,4},{4,8},{8,12},{12,16},{16,20},{20,24},{24,28},{28,32},{32,36}... | collective-permute-start | bytes 3080 | tf_op jit(solution)/shard_map/while/body/eval_jaxpr/ppermute | solution.py:14
  445.5 22.8 %collective-permute-start.3 = (f32[256,768]{1,0:T(8,128)}, f32[256,768]{1,0:T(8,128)}, u32[]{:S(2)}, u32[]{:S(2)}) collective-permute-start(f32[256,768]{1,0:T(8,128)} %get-tuple-element.479), channel_id=1, source_target_pairs={{0,4},{4,8},{8,12},{12,16},{16,20},{20,24},{24,28},{28,32},{32,36}... | collective-permute-start | bytes 2359304 | tf_op jit(solution)/shard_map/while/body/eval_jaxpr/ppermute | solution.py:14
  471.0 16.9 %collective-permute-start = (bf16[256,768]{1,0:T(8,128)(2,1)}, bf16[256,768]{1,0:T(8,128)(2,1)S(1)}, u32[]{:S(2)}, u32[]{:S(2)}) collective-permute-start(bf16[256,768]{1,0:T(8,128)(2,1)} %get-tuple-element.476), channel_id=1, source_target_pairs={{0,4},{4,8},{8,12},{12,16},{16,20},{20,24},{24,28},{28,32},{32,36}... | collective-permute-start | bytes 1179656 | tf_op jit(solution)/shard_map/while/body/eval_jaxpr/ppermute | solution.py:14
  471.0 15.7 %collective-permute-start.2 = (s32[256]{0:T(256)}, s32[256]{0:T(256)S(1)}, u32[]{:S(2)}, u32[]{:S(2)}) collective-permute-start(s32[256]{0:T(256)} %get-tuple-element.478), channel_id=1, source_target_pairs={{0,4},{4,8},{8,12},{12,16},{16,20},{20,24},{24,28},{28,32},{32,36}... | collective-permute-start | bytes 3080 | tf_op jit(solution)/shard_map/while/body/eval_jaxpr/ppermute | solution.py:14
  471.0 16.3 %collective-permute-start.1 = (s32[256]{0:T(256)}, s32[256]{0:T(256)S(1)}, u32[]{:S(2)}, u32[]{:S(2)}) collective-permute-start(s32[256]{0:T(256)} %get-tuple-element.477), channel_id=1, source_target_pairs={{0,4},{4,8},{8,12},{12,16},{16,20},{20,24},{24,28},{28,32},{32,36}... | collective-permute-start | bytes 3080 | tf_op jit(solution)/shard_map/while/body/eval_jaxpr/ppermute | solution.py:14
  471.0 23.9 %collective-permute-start.3 = (f32[256,768]{1,0:T(8,128)}, f32[256,768]{1,0:T(8,128)}, u32[]{:S(2)}, u32[]{:S(2)}) collective-permute-start(f32[256,768]{1,0:T(8,128)} %get-tuple-element.479), channel_id=1, source_target_pairs={{0,4},{4,8},{8,12},{12,16},{16,20},{20,24},{24,28},{28,32},{32,36}... | collective-permute-start | bytes 2359304 | tf_op jit(solution)/shard_map/while/body/eval_jaxpr/ppermute | solution.py:14
  499.2 15.8 %collective-permute-start.4 = (f32[256,768]{1,0:T(8,128)}, f32[256,768]{1,0:T(8,128)S(1)}, u32[]{:S(2)}, u32[]{:S(2)}) collective-permute-start(f32[256,768]{1,0:T(8,128)} %get-tuple-element.338), channel_id=1, source_target_pairs={{0,64},{4,68},{8,72},{12,76},{16,80},{20,84},{24,88},{28,92},{32,9... | collective-permute-start | bytes 2359304 | tf_op jit(solution)/shard_map/ppermute | solution.py:14
  (55 other events, 574.4 us)
Sparse Core Ops, SparseCore 0:
  10.9 27.4 all-gather.3
  499.4 60.4 reduce-scatter.1
where the time goes:
time: 570 us; the launch traced here: 569 us
  waiting for transfers between devices  371 us (65%)
  matrix products  105 us (18%)
  local copies, waits for them, and re-layouts  36.5 us (6%)
  blocking collectives  15.5 us (3%)
  between operations  14.7 us (3%)
  starting transfers between devices  13.6 us (2%)
  other arithmetic  11.5 us (2%)
    ppermute x65, waiting for transfers between devices, shifted(): return lax.ppermute(value, axis, pairs)  316 us
    dot_general x17, matrix products, slope_block(): jnp.einsum('qd,kd->qk', queries, keys, preferred_element_type=jnp.float32)  51.3 us
    reduce_scatter x1, waiting for transfers between devices, local(): owned = lax.psum_scatter(gathered, 'view', scatter_dimension=0, tiled=True)  44.9 us
    dot_general x16, matrix products, advance(): jnp.einsum('qk,qd->kd', slope, queries, preferred_element_type=jnp.float32)  42 us
    while x80, local copies, waits for them, and re-layouts  29.8 us
    ppermute x65, starting transfers between devices, shifted(): return lax.ppermute(value, axis, pairs)  13.5 us
  transfers between devices with their start and end apart: 67, of which 35 were waited for; matrix products, arithmetic and copies ran while one was open for 17% of the time, Pallas kernels for 0%

commit v1 on v0

v1 whole, which is shorter than its diff:
```python
import functools
import math

import jax
import jax.numpy as jnp
from jax import lax
from jax.experimental import pallas as pl
from jax.experimental.pallas import tpu as pltpu
from jax.sharding import PartitionSpec as P

D = 768
B = 256
H = B // 2
MESH = pl.DeviceIdType.MESH
NT = (((1,), (1,)), ((), ()))

SLOTS = [(0, 0), (1, 0), (3, 0), (0, 1), (0, 3), (2, 0), (1, 1), (1, 3)]
SLOTS += [(3, 1), (3, 3), (0, 2), (2, 1), (2, 3), (1, 2), (3, 2), (2, 2)]
SLOT = {rel: k for k, rel in enumerate(SLOTS)}

OPP, UP, DOWN, OWN = 0, B, 2 * B, 3 * B


def wrap(value):
    return lax.rem(value + 4, 4)


def device(x, y, z, core):
    x, y, z = wrap(x), wrap(y), wrap(z)
    return ((y * 4 + x) * 2 + lax.rem(z, 2), lax.div(z, 2) * 2 + core)


def kernel(x_ref, meta_ref, scale_ref, bias_ref, out_ref, keys, rows, acc, key_meta, line_meta, key_ids, row_ids,
           row_tiles, halves, wholes, send, recv):
    region = lax.axis_index("region")
    view = lax.axis_index("view")
    y, x = lax.div(region, 8), lax.rem(lax.div(region, 2), 4)
    z, core = lax.div(view, 2) * 2 + lax.rem(region, 2), lax.rem(view, 2)
    sibling = device(x, y, z, 1 - core)

    def first(step):
        return device(x + (1 - core) * step, y + core * step, z, core)

    def second(step):
        return device(x + core * step, y + (1 - core) * step, z, core)

    def line(step):
        return device(x, y, z + step, core)

    barrier = pltpu.get_barrier_semaphore()
    peers = [sibling] + [go(step) for go in (first, second, line) for step in (1, -1, 2)]
    for peer in peers:
        pl.semaphore_signal(barrier, inc=1, device_id=peer, device_id_type=MESH)
    pl.semaphore_wait(barrier, len(peers))

    copies = {}

    def start(name, src, dst, target):
        index = len(copies)
        copies[name] = pltpu.make_async_remote_copy(
            src_ref=src, dst_ref=dst, send_sem=send.at[index], recv_sem=recv.at[index],
            device_id=target, device_id_type=MESH,
        )
        copies[name].start()

    def arrived(*names):
        for name in names:
            copies[name].wait_recv()

    def slot(rel, whose=0, begin=0, count=B):
        return keys.at[pl.ds((2 * SLOT[rel] + whose) * B + begin, count)]

    def moved(rel, axis, step):
        return tuple((r - step * (i == axis)) % 4 for i, r in enumerate(rel))

    def whole(rel, axis, step):
        start(("w", axis, step, rel), x_ref if rel == (0, 0) else slot(rel), slot(moved(rel, axis, step)),
              (first, second)[axis](step))

    def half(rel, axis, step):
        begin = 0 if step == 1 else H
        start(("h", axis, step, rel), slot(rel, 0, begin, H), slot(moved(rel, axis, step), 0, begin, H),
              (first, second)[axis](step))

    def share(rel):
        start(("s", rel), x_ref if rel == (0, 0) else slot(rel), slot(rel, 1), sibling)

    def shared(*rels):
        arrived(*[("s", rel) for rel in rels])

    def from_whole(axis, *rels):
        for rel in rels:
            step = 1 if rel[axis] == 3 else -1
            arrived(("w", axis, step, moved(rel, axis, -step)))

    def from_halves(axis, rel):
        arrived(("h", axis, 1, moved(rel, axis, -1)), ("h", axis, -1, moved(rel, axis, 1)))

    mine = pl.ds(pl.multiple_of(((y * 4 + x) * 2 + core) * 8, 8), 8)
    chip = pl.ds(pl.multiple_of((y * 4 + x) * 16, 16), 16)
    lane = pl.ds(pl.multiple_of(y * 64, 64), 64)
    key_meta[mine, :] = meta_ref[...]
    start("ms", meta_ref, key_meta.at[mine], sibling)
    start("mu", meta_ref, line_meta.at[pl.ds(16, 8)], line(1))
    start("md", meta_ref, line_meta.at[pl.ds(8, 8)], line(-1))
    start("mo", meta_ref, line_meta.at[pl.ds(0, 8)], line(2))

    for axis in (0, 1):
        for step in (1, -1):
            whole((0, 0), axis, step)
    start("ru", x_ref, rows.at[pl.ds(DOWN, B)], line(1))
    start("rd", x_ref, rows.at[pl.ds(UP, B)], line(-1))
    share((0, 0))

    keys[0:B, :] = x_ref[...]
    rows[OWN:OWN + B, :] = x_ref[...]
    line_meta[24:32, :] = meta_ref[...]
    acc[...] = jnp.zeros_like(acc)

    def beside(step):
        return device(x + step, y, z, core)

    def across(step):
        return device(x, y + step, z, core)

    arrived("ms")
    for step in (1, -1, 2):
        start(("mx", step), key_meta.at[chip], key_meta.at[chip], beside(step))
    arrived(("mx", 1), ("mx", -1), ("mx", 2))
    for step in (1, -1, 2):
        start(("my", step), key_meta.at[lane], key_meta.at[lane], across(step))
    arrived("mu", "md", "mo")
    for block in range(4):
        for part in range(2):
            at = pl.ds(block * B + part * H, H)
            row = block * 8 + part
            row_ids[at, :] = jnp.broadcast_to(line_meta[row:row + 1, :], (H, H)).T
            row_tiles[at, :] = jnp.broadcast_to(line_meta[row + 2:row + 3, :], (H, H)).T
    arrived(("my", 1), ("my", -1), ("my", 2))
    for k, (a, b) in enumerate(SLOTS):
        for whose in range(2):
            owner = core + whose - 2 * core * whose
            kx = wrap(x + (1 - owner) * a + owner * b)
            ky = wrap(y + owner * a + (1 - owner) * b)
            tile = key_meta[pl.ds(pl.multiple_of(((ky * 4 + kx) * 2 + owner) * 8, 8), 8), :]
            for part in range(2):
                at = pl.ds((2 * k + whose) * B + part * H, H)
                key_ids[0:1, at] = tile[part:part + 1, :]
                key_ids[1:2, at] = tile[part + 2:part + 3, :]

    half_scale = scale_ref[0] * (0.5 / math.sqrt(D))
    half_bias = bias_ref[0] * 0.5

    def work(row, count, k, ks, diagonal=False):
        at, cols = pl.ds(row, count), pl.ds(2 * B * k, 2 * B * ks)
        block = keys[cols, :]
        logits = lax.dot_general(rows[at, :], block, NT, preferred_element_type=jnp.float32)
        curve = jnp.tanh(logits * half_scale + half_bias)
        same = row_ids[at, :][:, 0:1] == key_ids[0:1, cols]
        if diagonal:
            same &= lax.broadcasted_iota(jnp.int32, curve.shape, 0) != lax.broadcasted_iota(jnp.int32, curve.shape, 1)
        near = row_tiles[at, :][:, 0:1] == key_ids[1:2, cols]
        slope = curve + jnp.where(same, -1.0, 1.0)
        slope = jnp.where(near & ~same, 0.0, slope).astype(jnp.bfloat16)
        acc[at, :] += jnp.dot(slope, block, preferred_element_type=jnp.float32)

    shared((0, 0))
    work(OWN, B, 0, 1, diagonal=True)

    from_whole(0, (1, 0), (3, 0))
    for step in (1, -1):
        half(((3 if step == 1 else 1), 0), 0, step)
        whole((1, 0), 1, step)
        whole((3, 0), 1, step)
    from_whole(1, (0, 1), (0, 3))
    for step in (1, -1):
        half((0, 3 if step == 1 else 1), 1, step)
    arrived("ru", "rd")
    start("ou", rows.at[pl.ds(DOWN, H)], rows.at[pl.ds(OPP, H)], line(1))
    start("od", rows.at[pl.ds(UP + H, H)], rows.at[pl.ds(OPP + H, H)], line(-1))
    for rel in SLOTS[1:5]:
        share(rel)
    work(UP, 2 * B, 0, 1)
    shared(*SLOTS[1:5])
    work(UP, 3 * B, 1, 4)

    from_halves(0, (2, 0))
    for step in (1, -1):
        whole((2, 0), 1, step)
    from_whole(1, (1, 1), (1, 3))
    for step in (1, -1):
        half((1, 3 if step == 1 else 1), 1, step)
    for rel in SLOTS[5:8]:
        share(rel)
    arrived("ou", "od")
    work(OPP, B, 0, 5)
    shared(*SLOTS[5:8])
    work(OPP, 2 * B, 5, 3)

    from_whole(1, (3, 1), (3, 3))
    for step in (1, -1):
        half((3, 3 if step == 1 else 1), 1, step)
    from_halves(1, (0, 2))
    for rel in SLOTS[8:11]:
        share(rel)
    work(DOWN, 2 * B, 5, 3)
    shared(*SLOTS[8:11])
    work(OPP, 2 * B, 8, 3)

    from_whole(1, (2, 1), (2, 3))
    for step in (1, -1):
        half((2, 3 if step == 1 else 1), 1, step)
    for rel in SLOTS[11:13]:
        share(rel)
    work(DOWN, 2 * B, 8, 3)
    shared(*SLOTS[11:13])
    work(OPP, 2 * B, 11, 2)
    work(DOWN, 2 * B, 11, 2)

    from_halves(1, (1, 2))
    share((1, 2))
    from_halves(1, (3, 2))
    share((3, 2))
    from_halves(1, (2, 2))
    share((2, 2))
    shared(*SLOTS[13:16])
    work(OPP, B, 13, 3)
    start("hu", acc.at[pl.ds(OPP, H)], halves.at[0], line(1))
    start("hd", acc.at[pl.ds(OPP + H, H)], halves.at[1], line(-1))
    work(UP, B, 13, 3)
    work(DOWN, B, 13, 3)
    arrived("hu", "hd")
    acc[UP:UP + H, :] += halves[0]
    start("gu", acc.at[pl.ds(UP, B)], wholes.at[0], line(1))
    acc[DOWN + H:DOWN + B, :] += halves[1]
    start("gd", acc.at[pl.ds(DOWN, B)], wholes.at[1], line(-1))
    work(OWN, B, 13, 3)
    arrived("gu", "gd")
    out_ref[...] = (acc[OWN:OWN + B, :] + wholes[0] + wholes[1]) * (2.0 * half_scale)
    for copy in copies.values():
        copy.wait_send()


COPIES = 64


def local(embeddings, region_ids, tile_ids, logit_scale, logit_bias):
    meta = jnp.concatenate(
        [region_ids.reshape(2, H), tile_ids.reshape(2, H), jnp.zeros((4, H), jnp.int32)], axis=0
    )
    vmem, smem = pl.BlockSpec(memory_space=pltpu.VMEM), pl.BlockSpec(memory_space=pltpu.SMEM)
    return pl.pallas_call(
        kernel,
        out_shape=jax.ShapeDtypeStruct((B, D), jnp.float32),
        in_specs=[vmem, vmem, smem, smem],
        out_specs=vmem,
        scratch_shapes=[
            pltpu.VMEM((32 * B, D), jnp.bfloat16),
            pltpu.VMEM((4 * B, D), jnp.bfloat16),
            pltpu.VMEM((4 * B, D), jnp.float32),
            pltpu.VMEM((B, H), jnp.int32),
            pltpu.VMEM((32, H), jnp.int32),
            pltpu.VMEM((8, 32 * B), jnp.int32),
            pltpu.VMEM((4 * B, H), jnp.int32),
            pltpu.VMEM((4 * B, H), jnp.int32),
            pltpu.VMEM((2, H, D), jnp.float32),
            pltpu.VMEM((2, B, D), jnp.float32),
            pltpu.SemaphoreType.DMA((COPIES,)),
            pltpu.SemaphoreType.DMA((COPIES,)),
        ],
        compiler_params=pltpu.CompilerParams(
            collective_id=0, has_side_effects=True, vmem_limit_bytes=56 * 1024 * 1024
        ),
        name="pair_gradients",
    )(embeddings, meta, logit_scale, logit_bias)


def solution(mesh):
    placed = (P(("region", "view"), None), P(("region", "view")), P(("region", "view")), P(), P())
    return jax.shard_map(
        local, mesh=mesh, in_specs=placed, out_specs=P(("region", "view"), None), check_vma=False
    )
```

time: 570 us -> 92.9 us (0.16)
  waiting for transfers between devices: 371 us -> 0 us
  matrix products: 105 us -> 0 us
  Pallas kernels: 0 us -> 87.6 us
  local copies, waits for them, and re-layouts: 36.5 us -> 2.74 us
  blocking collectives: 15.5 us -> 0 us
  starting transfers between devices: 13.6 us -> 0 us
  between operations: 14.7 us -> 1.33 us
  other arithmetic: 11.5 us -> 0.66 us
    ppermute x65 -> x0, waiting for transfers between devices: 316 us -> none  [shifted(): return lax.ppermute(value, axis, pairs)]
    dot_general x51 -> x0, matrix products: 105 us -> none  [the longest x17 51.3 us: slope_block(): jnp.einsum('qd,kd->qk', queries, keys, preferred_element_type=jnp.float32)]
    pallas_call x0 -> x1, Pallas kernels: none -> 87.6 us  [local(): pl.pallas_call(kernel, out_shape=jax.ShapeDtypeStruct((B, D), jnp.float32...]
    reduce_scatter x1 -> x0, waiting for transfers between devices: 44.9 us -> none  [local(): owned = lax.psum_scatter(gathered, 'view', scatter_dimension=0, tiled=True)]
    while x80 -> x0, local copies, waits for them, and re-layouts: 29.8 us -> none
    all_gather x2 -> x0, blocking collectives: 15.5 us -> none  [the longest x1 8.51 us: local(): lax.all_gather(tile_ids, 'view', axis=0, tiled=True)]
    ppermute x65 -> x0, starting transfers between devices: 13.5 us -> none  [shifted(): return lax.ppermute(value, axis, pairs)]
    all_gather x1 -> x0, waiting for transfers between devices: 10.7 us -> none  [local(): lax.all_gather(embeddings, 'view', axis=0, tiled=True)]
  transfers between devices with their start and end apart: 67 -> 0, of which waited for: 35 -> 0; matrix products, arithmetic and copies ran while one was open for 17% -> 0% of each run, Pallas kernels for 0% -> 0%
where the time goes in v1:
time: 92.9 us; the launch traced here: 92.3 us
  Pallas kernels  87.6 us (94%)
  local copies, waits for them, and re-layouts  2.74 us (3%)
  between operations  1.33 us (1%)
    pallas_call x1, Pallas kernels, local(): pl.pallas_call(kernel, out_shape=jax.ShapeDtypeStruct((B, D), jnp.float32...  87.6 us
    unnamed x5, local copies, waits for them, and re-layouts  2.66 us

profile of v1, /device:TPU:1, one launch (start us, length us, event | category | flops | bytes accessed | tf_op | source)
XLA Modules:
  0.0 92.3 jit_solution(10941608947803911213)
XLA Ops:
  1.3 0.0 copy-start.1
  1.3 0.0 copy-start
  1.3 0.1 pad.2.clone
  1.4 0.6 copy-done.1
  2.0 0.0 copy-done
  2.0 0.7 add_add_fusion.meta_ref
  2.7 87.6 %pair_gradients.1 = f32[256,768]{1,0:T(8,128)} custom-call(bf16[256,768]{1,0:T(8,128)(2,1)} %x_ref.1, s32[8,128]{1,0:T(8,128)} %add_add_fusion.meta_ref, f32[1]{0:T(128)S(6)} %copy.7.scale_ref, f32[1]{0:T(128)S(6)} %copy.8.bias_ref), custom_call_target="tpu_custom_call" | custom-call | tf_op jit(solution)/shard_map/pair_gradients/pallas_call | solution.py:252
  90.2 2.1 %copy.9 = f32[256,768]{1,0:T(8,128)} copy(f32[256,768]{1,0:T(8,128)} %pair_gradients.1) | data formatting | bytes 1572864
  (1 shorter events, 0.0 us)
Async XLA Ops:
  1.3 0.7 copy-start.1
  1.3 0.7 copy-start

commit v2 on v1

v2 whole, which is shorter than its diff:
```python
import functools
import math

import jax
import jax.numpy as jnp
from jax import lax
from jax.experimental import pallas as pl
from jax.experimental.pallas import tpu as pltpu
from jax.sharding import PartitionSpec as P

D = 768
B = 256
H = B // 2
MESH = pl.DeviceIdType.MESH
NT = (((1,), (1,)), ((), ()))

SLOTS = [(0, 0), (1, 0), (3, 0), (0, 1), (0, 3), (2, 0), (1, 1), (1, 3)]
SLOTS += [(3, 1), (3, 3), (0, 2), (2, 1), (2, 3), (1, 2), (3, 2), (2, 2)]
SLOT = {rel: k for k, rel in enumerate(SLOTS)}

OPP, UP, DOWN, OWN = 0, B, 2 * B, 3 * B


def wrap(value):
    return lax.rem(value + 4, 4)


def device(x, y, z, core):
    x, y, z = wrap(x), wrap(y), wrap(z)
    return ((y * 4 + x) * 2 + lax.rem(z, 2), lax.div(z, 2) * 2 + core)


def kernel(x_ref, ids_ref, tiles_ref, scale_ref, bias_ref, out_ref, keys, rows, acc, key_meta, line_meta, key_ids,
           row_ids, row_tiles, coded, coded_top, landed, landed_top, local_sem, send, recv):
    region = lax.axis_index("region")
    view = lax.axis_index("view")
    y, x = lax.div(region, 8), lax.rem(lax.div(region, 2), 4)
    z, core = lax.div(view, 2) * 2 + lax.rem(region, 2), lax.rem(view, 2)
    sibling = device(x, y, z, 1 - core)

    def first(step):
        return device(x + (1 - core) * step, y + core * step, z, core)

    def second(step):
        return device(x + core * step, y + (1 - core) * step, z, core)

    def line(step):
        return device(x, y, z + step, core)

    fetch = pltpu.make_async_copy(x_ref, keys.at[pl.ds(0, B)], local_sem)
    fetch.start()
    barrier = pltpu.get_barrier_semaphore()
    peers = [sibling] + [go(step) for go in (first, second, line) for step in (1, -1)]
    for peer in peers:
        pl.semaphore_signal(barrier, inc=1, device_id=peer, device_id_type=MESH)
    for part in range(2):
        for held in (key_meta.at[0, part], line_meta.at[3, part]):
            held[0:1, :] = ids_ref[part:part + 1, :]
            held[1:2, :] = tiles_ref[part:part + 1, :]
    fetch.wait()
    pl.semaphore_wait(barrier, len(peers))

    copies = {}

    def start(name, src, dst, target):
        index = len(copies)
        copies[name] = pltpu.make_async_remote_copy(
            src_ref=src, dst_ref=dst, send_sem=send.at[index], recv_sem=recv.at[index],
            device_id=target, device_id_type=MESH,
        )
        copies[name].start()

    def arrived(*names):
        for name in names:
            copies[name].wait_recv()

    def slot(rel, whose=0, begin=0, count=B):
        return keys.at[pl.ds((2 * SLOT[rel] + whose) * B + begin, count)]

    def meta(rel, whose=0):
        return key_meta.at[2 * SLOT[rel] + whose]

    def moved(rel, axis, step):
        return tuple((r - step * (i == axis)) % 4 for i, r in enumerate(rel))

    def whole(rel, axis, step):
        target = (first, second)[axis](step)
        to = moved(rel, axis, step)
        start(("mw", axis, step, rel), meta(rel), meta(to), target)
        start(("w", axis, step, rel), slot(rel), slot(to), target)

    def half(rel, axis, step):
        target = (first, second)[axis](step)
        to = moved(rel, axis, step)
        begin = 0 if step == 1 else H
        if step == 1:
            start(("mh", axis, rel), meta(rel), meta(to), target)
        start(("h", axis, step, rel), slot(rel, 0, begin, H), slot(to, 0, begin, H), target)

    def share(*rels):
        for rel in rels:
            start(("ms", rel), meta(rel), meta(rel, 1), sibling)
            start(("s", rel), slot(rel), slot(rel, 1), sibling)

    def shared(*rels):
        for rel in rels:
            arrived(("ms", rel), ("s", rel))
        for rel in rels:
            for whose in range(2):
                at = 2 * SLOT[rel] + whose
                for part in range(2):
                    key_ids[0:2, pl.ds(at * B + part * H, H)] = key_meta[at, part]

    def from_whole(axis, *rels):
        for rel in rels:
            step = 1 if rel[axis] == 3 else -1
            arrived(("mw", axis, step, moved(rel, axis, -step)), ("w", axis, step, moved(rel, axis, -step)))

    def from_halves(axis, rel):
        arrived(("mh", axis, moved(rel, axis, -1)))
        arrived(("h", axis, 1, moved(rel, axis, -1)), ("h", axis, -1, moved(rel, axis, 1)))

    for axis in (0, 1):
        for step in (1, -1):
            whole((0, 0), axis, step)
    start("mu", line_meta.at[3], line_meta.at[2], line(1))
    start("md", line_meta.at[3], line_meta.at[1], line(-1))
    start("ru", keys.at[pl.ds(0, B)], rows.at[pl.ds(DOWN, B)], line(1))
    start("rd", keys.at[pl.ds(0, B)], rows.at[pl.ds(UP, B)], line(-1))
    share((0, 0))
    rows[OWN:OWN + B, :] = keys[0:B, :]
    acc[...] = jnp.zeros_like(acc)

    def label_rows(*blocks):
        for block in blocks:
            for part in range(2):
                at = pl.ds(block * B + part * H, H)
                held = line_meta[block, part]
                row_ids[at, :] = jnp.broadcast_to(held[0:1, :], (H, H)).T
                row_tiles[at, :] = jnp.broadcast_to(held[1:2, :], (H, H)).T

    half_scale = scale_ref[0] * (0.5 / math.sqrt(D))
    half_bias = bias_ref[0] * 0.5

    def work(row, count, k, ks, diagonal=False):
        at, cols = pl.ds(row, count), pl.ds(2 * B * k, 2 * B * ks)
        block = keys[cols, :]
        logits = lax.dot_general(rows[at, :], block, NT, preferred_element_type=jnp.float32)
        curve = jnp.tanh(logits * half_scale + half_bias)
        same = row_ids[at, :][:, 0:1] == key_ids[0:1, cols]
        if diagonal:
            same &= lax.broadcasted_iota(jnp.int32, curve.shape, 0) != lax.broadcasted_iota(jnp.int32, curve.shape, 1)
        near = row_tiles[at, :][:, 0:1] == key_ids[1:2, cols]
        slope = curve + jnp.where(same, -1.0, 1.0)
        slope = jnp.where(near & ~same, 0.0, slope).astype(jnp.bfloat16)
        acc[at, :] += jnp.dot(slope, block, preferred_element_type=jnp.float32)

    def pass_on(piece, row, step):
        sums = acc[pl.ds(row, H), :].reshape(H // 8, 8, D)
        top = jnp.maximum(jnp.max(jnp.abs(sums), axis=0), 1e-30)
        coded_top[piece] = top
        code = jnp.floor(sums * (32767.0 / top)[None] + 0.5).astype(jnp.int32)
        coded[piece] = code.reshape(H, D).astype(jnp.int16)
        start(("t", piece), coded_top.at[piece], landed_top.at[piece], line(step))
        start(("q", piece), coded.at[piece], landed.at[piece], line(step))

    def take_in(piece, row):
        arrived(("t", piece), ("q", piece))
        sums = landed[piece].astype(jnp.int32).astype(jnp.float32).reshape(H // 8, 8, D)
        sums = sums * (landed_top[piece] * (1.0 / 32767.0))[None]
        acc[pl.ds(row, H), :] += sums.reshape(H, D)

    label_rows(3)
    shared((0, 0))
    work(OWN, B, 0, 1, diagonal=True)

    from_whole(0, (1, 0), (3, 0))
    for step in (1, -1):
        half(((3 if step == 1 else 1), 0), 0, step)
        whole((1, 0), 1, step)
        whole((3, 0), 1, step)
    from_whole(1, (0, 1), (0, 3))
    for step in (1, -1):
        half((0, 3 if step == 1 else 1), 1, step)
    share(*SLOTS[1:5])
    arrived("mu", "md", "ru", "rd")
    start("mo", line_meta.at[2], line_meta.at[0], line(1))
    start("ou", rows.at[pl.ds(DOWN, H)], rows.at[pl.ds(OPP, H)], line(1))
    start("od", rows.at[pl.ds(UP + H, H)], rows.at[pl.ds(OPP + H, H)], line(-1))
    label_rows(1, 2)
    work(UP, 2 * B, 0, 1)
    shared(*SLOTS[1:5])
    work(UP, 2 * B, 1, 4)

    arrived("mo", "ou", "od")
    label_rows(0)
    from_halves(0, (2, 0))
    for step in (1, -1):
        whole((2, 0), 1, step)
    work(OPP, B, 0, 5)
    from_whole(1, (1, 1), (1, 3))
    for step in (1, -1):
        half((1, 3 if step == 1 else 1), 1, step)
    share(*SLOTS[5:8])
    work(OWN, B, 1, 4)
    shared(*SLOTS[5:8])
    work(UP, 2 * B, 5, 3)

    from_whole(1, (3, 1), (3, 3))
    for step in (1, -1):
        half((3, 3 if step == 1 else 1), 1, step)
    from_halves(1, (0, 2))
    share(*SLOTS[8:11])
    work(OPP, B, 5, 3)
    shared(*SLOTS[8:11])
    work(UP, 2 * B, 8, 3)

    from_whole(1, (2, 1), (2, 3))
    for step in (1, -1):
        half((2, 3 if step == 1 else 1), 1, step)
    share(*SLOTS[11:13])
    work(OPP, B, 8, 3)
    shared(*SLOTS[11:13])
    work(UP, 2 * B, 11, 2)

    from_halves(1, (1, 2))
    from_halves(1, (3, 2))
    share(*SLOTS[13:15])
    work(OPP, B, 11, 2)
    shared(*SLOTS[13:15])
    work(UP, 2 * B, 13, 2)

    from_halves(1, (2, 2))
    share((2, 2))
    work(OPP, B, 13, 2)
    shared((2, 2))
    work(OPP, B, 15, 1)
    pass_on(0, OPP, 1)
    pass_on(1, OPP + H, -1)
    work(UP, 2 * B, 15, 1)
    pass_on(2, UP + H, 1)
    pass_on(3, DOWN, -1)
    work(OWN, B, 5, 6)
    take_in(0, UP)
    pass_on(4, UP, 1)
    take_in(1, DOWN + H)
    pass_on(5, DOWN + H, -1)
    work(OWN, B, 11, 5)
    take_in(2, OWN + H)
    take_in(3, OWN)
    take_in(4, OWN)
    take_in(5, OWN + H)
    out_ref[...] = acc[OWN:OWN + B, :]
    for copy in copies.values():
        copy.wait_send()


COPIES = 112


def local(embeddings, region_ids, tile_ids, logit_scale, logit_bias):
    vmem, smem = pl.BlockSpec(memory_space=pltpu.VMEM), pl.BlockSpec(memory_space=pltpu.SMEM)
    sums = pl.pallas_call(
        kernel,
        out_shape=jax.ShapeDtypeStruct((B, D), jnp.float32),
        in_specs=[pl.BlockSpec(memory_space=pl.ANY), vmem, vmem, smem, smem],
        out_specs=vmem,
        scratch_shapes=[
            pltpu.VMEM((32 * B, D), jnp.bfloat16),
            pltpu.VMEM((4 * B, D), jnp.bfloat16),
            pltpu.VMEM((4 * B, D), jnp.float32),
            pltpu.VMEM((32, 2, 2, H), jnp.int32),
            pltpu.VMEM((4, 2, 2, H), jnp.int32),
            pltpu.VMEM((8, 32 * B), jnp.int32),
            pltpu.VMEM((4 * B, H), jnp.int32),
            pltpu.VMEM((4 * B, H), jnp.int32),
            pltpu.VMEM((6, H, D), jnp.int16),
            pltpu.VMEM((6, 8, D), jnp.float32),
            pltpu.VMEM((6, H, D), jnp.int16),
            pltpu.VMEM((6, 8, D), jnp.float32),
            pltpu.SemaphoreType.DMA,
            pltpu.SemaphoreType.DMA((COPIES,)),
            pltpu.SemaphoreType.DMA((COPIES,)),
        ],
        compiler_params=pltpu.CompilerParams(
            collective_id=0, has_side_effects=True, vmem_limit_bytes=56 * 1024 * 1024
        ),
        name="pair_gradients",
    )(embeddings, region_ids.reshape(2, H), tile_ids.reshape(2, H), logit_scale, logit_bias)
    return sums * (logit_scale[0] * (1.0 / math.sqrt(D)))


def solution(mesh):
    placed = (P(("region", "view"), None), P(("region", "view")), P(("region", "view")), P(), P())
    return jax.shard_map(
        local, mesh=mesh, in_specs=placed, out_specs=P(("region", "view"), None), check_vma=False
    )
```

time: 92.9 us -> 75.2 us (0.81)
  Pallas kernels: 87.6 us -> 71.6 us
  local copies, waits for them, and re-layouts: 2.74 us -> 0 us
  other arithmetic: 0.66 us -> 2.07 us
    pallas_call x1, Pallas kernels: 87.6 us -> 71.6 us  [local(): pl.pallas_call(kernel, out_shape=jax.ShapeDtypeStruct((B, D), jnp.float32...]
    unnamed x5 -> x0, local copies, waits for them, and re-layouts: 2.66 us -> none
    mul x0 -> x1, other arithmetic: none -> 2.07 us  [local(): return sums * (logit_scale[0] * (1.0 / math.sqrt(D)))]
where the time goes in v2:
time: 75.2 us; the launch traced here: 75 us
  Pallas kernels  71.6 us (95%)
  other arithmetic  2.07 us (3%)
  between operations  1.31 us (2%)
    pallas_call x1, Pallas kernels, local(): pl.pallas_call(kernel, out_shape=jax.ShapeDtypeStruct((B, D), jnp.float32...  71.6 us
    mul x1, other arithmetic, local(): return sums * (logit_scale[0] * (1.0 / math.sqrt(D)))  2.07 us

profile of v2, /device:TPU:1, one launch (start us, length us, event | category | flops | bytes accessed | tf_op | source)
XLA Modules:
  0.0 75.0 jit_solution(2313169202185001510)
XLA Ops:
  1.3 71.6 %pair_gradients.1 = f32[256,768]{1,0:T(8,128)} custom-call(bf16[256,768]{1,0:T(8,128)(2,1)} %x_ref.1, s32[2,128]{1,0:T(2,128)} %bitcast.3, s32[2,128]{1,0:T(2,128)} %bitcast.4, f32[1]{0:T(128)S(6)} %copy.6.scale_ref, f32[1]{0:T(128)S(6)} %copy.7.bias_ref), custom_call_target="tpu_custom_call" | custom-call | tf_op jit(solution)/shard_map/pair_gradients/pallas_call | solution.py:263
  72.9 2.1 %broadcast_multiply_fusion = f32[256,768]{1,0:T(8,128)} fusion(f32[256,768]{1,0:T(8,128)} %pair_gradients.1, f32[]{:T(128)} %bitcast.2), kind=kLoop, calls=%fused_computation | loop fusion | flops 196608 | bytes 1572868 | tf_op jit(solution)/shard_map/mul | solution.py:290

commit v3 on v2

v3 whole, which is shorter than its diff:
```python
import functools
import math

import jax
import jax.numpy as jnp
from jax import lax
from jax.experimental import pallas as pl
from jax.experimental.pallas import tpu as pltpu
from jax.sharding import PartitionSpec as P

D = 768
B = 256
H = B // 2
MESH = pl.DeviceIdType.MESH
NT = (((1,), (1,)), ((), ()))

SLOTS = [(0, 0), (1, 0), (3, 0), (0, 1), (0, 3), (2, 0), (0, 2), (1, 1)]
SLOTS += [(1, 3), (3, 1), (3, 3), (2, 1), (2, 3), (1, 2), (3, 2), (2, 2)]
SLOT = {rel: k for k, rel in enumerate(SLOTS)}

OPP, UP, DOWN, OWN = (0, H), (B, 2 * B), (B + H, 2 * B + H), (3 * B, 3 * B + H)
LINE = (OPP, UP, DOWN, OWN)


def place(k, whose, begin=0):
    if 1 <= k <= 4:
        return 2 * B + begin * 8 + (k - 1) * B + whose * H
    return (2 * k + whose) * B + begin


def wrap(value):
    return lax.rem(value + 4, 4)


def device(x, y, z, core):
    x, y, z = wrap(x), wrap(y), wrap(z)
    return ((y * 4 + x) * 2 + lax.rem(z, 2), lax.div(z, 2) * 2 + core)


def kernel(x_ref, ids_ref, tiles_ref, scale_ref, bias_ref, out_ref, own_ids, keys, rows, acc, key_meta, line_meta,
           key_ids, row_ids, row_tiles, coded, coded_top, landed, landed_top, local_sem, send, recv):
    region = lax.axis_index("region")
    view = lax.axis_index("view")
    y, x = lax.div(region, 8), lax.rem(lax.div(region, 2), 4)
    z, core = lax.div(view, 2) * 2 + lax.rem(region, 2), lax.rem(view, 2)
    sibling = device(x, y, z, 1 - core)

    def first(step):
        return device(x + (1 - core) * step, y + core * step, z, core)

    def second(step):
        return device(x + core * step, y + (1 - core) * step, z, core)

    def line(step):
        return device(x, y, z + step, core)

    fetches = [
        pltpu.make_async_copy(x_ref, keys.at[pl.ds(0, B)], local_sem.at[0]),
        pltpu.make_async_copy(ids_ref, own_ids.at[0], local_sem.at[1]),
        pltpu.make_async_copy(tiles_ref, own_ids.at[1], local_sem.at[2]),
    ]
    for fetch in fetches:
        fetch.start()
    barrier = pltpu.get_barrier_semaphore()
    peers = [sibling] + [go(step) for go in (first, second, line) for step in (1, -1)]
    for peer in peers:
        pl.semaphore_signal(barrier, inc=1, device_id=peer, device_id_type=MESH)
    for fetch in fetches:
        fetch.wait()
    for part in range(2):
        for held in (key_meta.at[0, part], line_meta.at[3, part]):
            held[0:1, :] = own_ids[0, part:part + 1, :]
            held[1:2, :] = own_ids[1, part:part + 1, :]
    pl.semaphore_wait(barrier, len(peers))

    copies = {}

    def start(name, src, dst, target):
        index = len(copies)
        copies[name] = pltpu.make_async_remote_copy(
            src_ref=src, dst_ref=dst, send_sem=send.at[index], recv_sem=recv.at[index],
            device_id=target, device_id_type=MESH,
        )
        copies[name].start()

    def arrived(*names):
        for name in names:
            copies[name].wait_recv()

    def slot(rel, whose=0, begin=0, count=B):
        return keys.at[pl.ds(place(SLOT[rel], whose, begin), count)]

    def meta(rel, whose=0):
        return key_meta.at[2 * SLOT[rel] + whose]

    def moved(rel, axis, step):
        return tuple((r - step * (i == axis)) % 4 for i, r in enumerate(rel))

    def ids_on(rel, axis, step):
        start(("m", axis, step, rel), meta(rel), meta(moved(rel, axis, step)), (first, second)[axis](step))

    def send_on(rel, axis, step, part=None):
        begin, count = (0, B) if part is None else (part * H, H)
        start(("w", axis, step, rel, part), slot(rel, 0, begin, count),
              slot(moved(rel, axis, step), 0, begin, count), (first, second)[axis](step))

    def came(axis, rel, part=None):
        if rel[axis] == 2:
            step = 1 if part == 0 else -1
        else:
            step = 1 if rel[axis] == 3 else -1
        arrived(("w", axis, step, moved(rel, axis, -step), part))

    def ids_came(axis, *rels):
        for rel in rels:
            step = -1 if rel[axis] == 1 else 1
            arrived(("m", axis, step, moved(rel, axis, -step)))

    def share(rel, part=None):
        begin, count = (0, B) if part is None else (part * H, H)
        start(("s", rel, part), slot(rel, 0, begin, count), slot(rel, 1, begin, count), sibling)

    def share_ids(*rels):
        for rel in rels:
            start(("ms", rel), meta(rel), meta(rel, 1), sibling)

    def shared(*wanted):
        for want in wanted:
            rel, parts = (want[0], (want[1],)) if isinstance(want[0], tuple) else (want, (0, 1))
            if 0 in parts:
                arrived(("ms", rel))
            arrived(*[("s", rel, part) for part in (*parts, None) if ("s", rel, part) in copies])
            for whose in range(2):
                at = 2 * SLOT[rel] + whose
                for part in parts:
                    key_ids[0:2, pl.ds(place(SLOT[rel], whose, part * H), H)] = key_meta[at, part]

    here = (0, 0)
    for axis in (0, 1):
        for step in (1, -1):
            ids_on(here, axis, step)
    start("mu", line_meta.at[3], line_meta.at[2], line(1))
    start("md", line_meta.at[3], line_meta.at[1], line(-1))
    for part in range(2):
        for axis in (0, 1):
            for step in (1, -1):
                send_on(here, axis, step, part)
        at = pl.ds(part * H, H)
        start(("ru", part), keys.at[at], rows.at[pl.ds(DOWN[part], H)], line(1))
        start(("rd", part), keys.at[at], rows.at[pl.ds(UP[part], H)], line(-1))
    share_ids(here)
    share(here)
    rows[OWN[0]:OWN[0] + B, :] = keys[0:B, :]
    acc[...] = jnp.zeros_like(acc)

    def label_rows(*blocks):
        for block in blocks:
            for part in range(2):
                at = pl.ds(LINE[block][part], H)
                held = line_meta[block, part]
                row_ids[at, :] = jnp.broadcast_to(held[0:1, :], (H, H)).T
                row_tiles[at, :] = jnp.broadcast_to(held[1:2, :], (H, H)).T

    half_scale = scale_ref[0] * (0.5 / math.sqrt(D))
    half_bias = bias_ref[0] * 0.5

    def work(row, begin, end, diagonal=False):
        at, cols = pl.ds(row, B), pl.ds(begin, end - begin)
        block = keys[cols, :]
        logits = lax.dot_general(rows[at, :], block, NT, preferred_element_type=jnp.float32)
        curve = jnp.tanh(logits * half_scale + half_bias)
        same = row_ids[at, :][:, 0:1] == key_ids[0:1, cols]
        if diagonal:
            same &= lax.broadcasted_iota(jnp.int32, curve.shape, 0) != lax.broadcasted_iota(jnp.int32, curve.shape, 1)
        near = row_tiles[at, :][:, 0:1] == key_ids[1:2, cols]
        slope = curve + jnp.where(same, -1.0, 1.0)
        slope = jnp.where(near & ~same, 0.0, slope).astype(jnp.bfloat16)
        acc[at, :] += jnp.dot(slope, block, preferred_element_type=jnp.float32)

    def pass_on(piece, row, step):
        sums = acc[pl.ds(row, H), :].reshape(H // 8, 8, D)
        top = jnp.maximum(jnp.max(jnp.abs(sums), axis=0), 1e-30)
        coded_top[piece] = top
        code = jnp.floor(sums * (32767.0 / top)[None] + 0.5).astype(jnp.int32)
        coded[piece] = code.reshape(H, D).astype(jnp.int16)
        start(("t", piece), coded_top.at[piece], landed_top.at[piece], line(step))
        start(("q", piece), coded.at[piece], landed.at[piece], line(step))

    def take_in(piece, row):
        arrived(("t", piece), ("q", piece))
        sums = landed[piece].astype(jnp.int32).astype(jnp.float32).reshape(H // 8, 8, D)
        sums = sums * (landed_top[piece] * (1.0 / 32767.0))[None]
        acc[pl.ds(row, H), :] += sums.reshape(H, D)

    def pair(k):
        return SLOTS[k], SLOTS[k + 1]

    def two_hops(rel):
        ids_came(1, rel)
        share_ids(rel)
        for part in range(2):
            came(1, rel, part)
            share(rel, part)

    def beside(rel):
        up, down = (rel, 3), (rel, 1)
        ids_came(1, up, down)
        ids_on(up, 1, 1)
        parts = [None] if rel == 2 else [0, 1]
        for part in parts:
            came(1, up, part)
        send_on(up, 1, 1, 0)
        for part in parts:
            came(1, down, part)
        send_on(down, 1, -1, 1)
        share_ids(down, up)
        share(down)
        share(up)

    def unit(k):
        return 2 * B * k

    opp, near, far, own = 0, B, 2 * B, 3 * B
    near_keys, far_keys = unit(3), unit(5)

    label_rows(3)
    shared(here)
    work(own, 0, unit(1), diagonal=True)

    ids_came(0, *pair(1))
    for rel in pair(1):
        came(0, rel, 0)
    send_on((3, 0), 0, 1, 0)
    for rel in pair(1):
        for step in (1, -1):
            ids_on(rel, 1, step)
            send_on(rel, 1, step, 0)
    ids_on((3, 0), 0, 1)
    ids_came(1, *pair(3))
    for rel in pair(3):
        came(1, rel, 0)
    ids_on((0, 3), 1, 1)
    send_on((0, 3), 1, 1, 0)
    share_ids(*SLOTS[1:5])
    for rel in SLOTS[1:5]:
        share(rel, 0)
    arrived("mu", "md")
    start("mo", line_meta.at[2], line_meta.at[0], line(1))
    arrived(("ru", 0), ("rd", 0))
    start("ou", rows.at[pl.ds(DOWN[0], H)], rows.at[pl.ds(OPP[0], H)], line(1))
    label_rows(1, 2)
    shared(*[(rel, 0) for rel in SLOTS[1:5]])
    work(near, 0, near_keys)

    for rel in pair(1):
        came(0, rel, 1)
    send_on((1, 0), 0, -1, 1)
    for rel in pair(3):
        came(1, rel, 1)
    send_on((0, 1), 1, -1, 1)
    for rel in pair(1):
        for step in (1, -1):
            send_on(rel, 1, step, 1)
    for rel in SLOTS[1:5]:
        share(rel, 1)
    arrived(("ru", 1), ("rd", 1))
    start("od", rows.at[pl.ds(UP[1], H)], rows.at[pl.ds(OPP[1], H)], line(-1))
    work(own, unit(1), near_keys)
    shared(*[(rel, 1) for rel in SLOTS[1:5]])
    work(near, near_keys, far_keys)
    work(far, 0, far_keys)

    arrived("mo", "ou", "od")
    label_rows(0)
    ids_came(0, (2, 0))
    for part in range(2):
        came(0, (2, 0), part)
    for step in (1, -1):
        ids_on((2, 0), 1, step)
        send_on((2, 0), 1, step)
    share_ids((2, 0))
    share((2, 0))
    work(opp, 0, far_keys)
    two_hops((0, 2))
    work(own, near_keys, far_keys)
    beside(1)

    def others(k):
        for row in (opp, near, far):
            work(row, unit(k), unit(k + 2))

    shared(*pair(5))
    others(5)
    beside(3)
    shared(*pair(7))
    others(7)
    shared(*pair(9))
    others(9)
    beside(2)
    work(own, unit(5), unit(9))
    two_hops((1, 2))
    two_hops((3, 2))
    shared(*pair(11))
    others(11)
    two_hops((2, 2))
    shared(*pair(13))
    work(opp, unit(13), unit(15))
    shared((2, 2))

    work(opp, unit(15), unit(16))
    pass_on(0, OPP[0], 1)
    pass_on(1, OPP[1], -1)
    work(near, unit(13), unit(16))
    work(far, unit(13), unit(16))
    pass_on(2, UP[1], 1)
    pass_on(3, DOWN[0], -1)
    work(own, unit(9), unit(13))
    work(own, unit(13), unit(16))
    take_in(0, UP[0])
    pass_on(4, UP[0], 1)
    take_in(1, DOWN[1])
    pass_on(5, DOWN[1], -1)
    take_in(2, OWN[1])
    take_in(3, OWN[0])
    take_in(4, OWN[0])
    take_in(5, OWN[1])
    out_ref[...] = acc[own:own + B, :]
    for copy in copies.values():
        copy.wait_send()


COPIES = 128


def local(embeddings, region_ids, tile_ids, logit_scale, logit_bias):
    hbm, vmem, smem = (pl.BlockSpec(memory_space=space) for space in (pltpu.HBM, pltpu.VMEM, pltpu.SMEM))
    sums = pl.pallas_call(
        kernel,
        out_shape=jax.ShapeDtypeStruct((B, D), jnp.float32),
        in_specs=[hbm, hbm, hbm, smem, smem],
        out_specs=vmem,
        scratch_shapes=[
            pltpu.VMEM((2, 2, H), jnp.int32),
            pltpu.VMEM((32 * B, D), jnp.bfloat16),
            pltpu.VMEM((4 * B, D), jnp.bfloat16),
            pltpu.VMEM((4 * B, D), jnp.float32),
            pltpu.VMEM((32, 2, 2, H), jnp.int32),
            pltpu.VMEM((4, 2, 2, H), jnp.int32),
            pltpu.VMEM((8, 32 * B), jnp.int32),
            pltpu.VMEM((4 * B, H), jnp.int32),
            pltpu.VMEM((4 * B, H), jnp.int32),
            pltpu.VMEM((6, H, D), jnp.int16),
            pltpu.VMEM((6, 8, D), jnp.float32),
            pltpu.VMEM((6, H, D), jnp.int16),
            pltpu.VMEM((6, 8, D), jnp.float32),
            pltpu.SemaphoreType.DMA((3,)),
            pltpu.SemaphoreType.DMA((COPIES,)),
            pltpu.SemaphoreType.DMA((COPIES,)),
        ],
        compiler_params=pltpu.CompilerParams(
            collective_id=0, has_side_effects=True, vmem_limit_bytes=36 * 1024 * 1024
        ),
        name="pair_gradients",
    )(embeddings, region_ids.reshape(2, H), tile_ids.reshape(2, H), logit_scale, logit_bias)
    return sums * (logit_scale[0] * (1.0 / math.sqrt(D)))


def solution(mesh):
    placed = (P(("region", "view"), None), P(("region", "view")), P(("region", "view")), P(), P())
    return jax.shard_map(
        local, mesh=mesh, in_specs=placed, out_specs=P(("region", "view"), None), check_vma=False
    )
```

time: 75.2 us -> 70.8 us (0.941)
  Pallas kernels: 71.6 us -> 66.7 us
  local copies, waits for them, and re-layouts: 0 us -> 1.67 us
  other arithmetic: 2.07 us -> 0.93 us
    pallas_call x1, Pallas kernels: 71.6 us -> 66.7 us  [local(): pl.pallas_call(kernel, out_shape=jax.ShapeDtypeStruct((B, D), jnp.float32...]
    unnamed x0 -> x6, local copies, waits for them, and re-layouts: none -> 1.67 us
    mul x1, other arithmetic: 2.07 us -> 0.93 us  [local(): return sums * (logit_scale[0] * (1.0 / math.sqrt(D)))]
where the time goes in v3:
time: 70.8 us; the launch traced here: 70.6 us
  Pallas kernels  66.7 us (94%)
  local copies, waits for them, and re-layouts  1.67 us (2%)
  between operations  1.33 us (2%)
  other arithmetic  0.93 us (1%)
    pallas_call x1, Pallas kernels, local(): pl.pallas_call(kernel, out_shape=jax.ShapeDtypeStruct((B, D), jnp.float32...  66.7 us
    unnamed x6, local copies, waits for them, and re-layouts  1.67 us

profile of v3, /device:TPU:1, one launch (start us, length us, event | category | flops | bytes accessed | tf_op | source)
XLA Modules:
  0.0 70.6 jit_solution(14901221795838328755)
XLA Ops:
  1.3 0.0 copy-start.2
  1.3 0.0 copy-start.1
  1.3 0.7 copy-done.2
  2.0 0.0 copy-done.1
  2.0 0.0 copy-start
  2.0 1.0 %copy-done = bf16[256,768]{1,0:T(8,128)(2,1)S(1)} copy-done((bf16[256,768]{1,0:T(8,128)(2,1)S(1)}, bf16[256,768]{1,0:T(8,128)(2,1)}, u32[]{:S(2)}) %copy-start) | copy-done | bytes 393240
  3.0 66.7 %pair_gradients.1 = f32[256,768]{1,0:T(8,128)S(1)} custom-call(bf16[256,768]{1,0:T(8,128)(2,1)S(1)} %copy-done, s32[2,128]{1,0:T(2,128)S(1)} %bitcast.3, s32[2,128]{1,0:T(2,128)S(1)} %bitcast.4, f32[1]{0:T(128)S(6)} %copy.6.scale_ref, f32[1]{0:T(128)S(6)} %copy.7.bias_ref), custom_call_target="tpu_custom_call" | custom-call | tf_op jit(solution)/shard_map/pair_gradients/pallas_call | solution.py:337
  69.7 0.9 %broadcast_multiply_fusion = f32[256,768]{1,0:T(8,128)} fusion(f32[256,768]{1,0:T(8,128)S(1)} %pair_gradients.1, f32[]{:T(128)} %bitcast.2), kind=kLoop, calls=%fused_computation | loop fusion | flops 196608 | bytes 1572868 | tf_op jit(solution)/shard_map/mul | solution.py:365
Async XLA Ops:
  1.3 0.7 copy-start.2
  1.3 0.7 copy-start.1
  2.0 1.0 %copy-start = (bf16[256,768]{1,0:T(8,128)(2,1)S(1)}, bf16[256,768]{1,0:T(8,128)(2,1)}, u32[]{:S(2)}) copy-start(bf16[256,768]{1,0:T(8,128)(2,1)} %x_ref.1) | copy-start | bytes 1179652

commit v4 on v3

--- a/solution.py
+++ b/solution.py
@@ -14,8 +14,8 @@
 MESH = pl.DeviceIdType.MESH
 NT = (((1,), (1,)), ((), ()))
 
-SLOTS = [(0, 0), (1, 0), (3, 0), (0, 1), (0, 3), (2, 0), (0, 2), (1, 1)]
-SLOTS += [(1, 3), (3, 1), (3, 3), (2, 1), (2, 3), (1, 2), (3, 2), (2, 2)]
+SLOTS = [(0, 0), (1, 0), (3, 0), (0, 1), (0, 3), (2, 0), (1, 1), (1, 3)]
+SLOTS += [(3, 1), (3, 3), (2, 1), (2, 3), (0, 2), (1, 2), (3, 2), (2, 2)]
 SLOT = {rel: k for k, rel in enumerate(SLOTS)}
 
 OPP, UP, DOWN, OWN = (0, H), (B, 2 * B), (B + H, 2 * B + H), (3 * B, 3 * B + H)
@@ -186,11 +186,13 @@
         start(("t", piece), coded_top.at[piece], landed_top.at[piece], line(step))
         start(("q", piece), coded.at[piece], landed.at[piece], line(step))
 
-    def take_in(piece, row):
+    def decoded(piece):
         arrived(("t", piece), ("q", piece))
         sums = landed[piece].astype(jnp.int32).astype(jnp.float32).reshape(H // 8, 8, D)
-        sums = sums * (landed_top[piece] * (1.0 / 32767.0))[None]
-        acc[pl.ds(row, H), :] += sums.reshape(H, D)
+        return (sums * (landed_top[piece] * (1.0 / 32767.0))[None]).reshape(H, D)
+
+    def take_in(piece, row):
+        acc[pl.ds(row, H), :] += decoded(piece)
 
     def pair(k):
         return SLOTS[k], SLOTS[k + 1]
@@ -239,8 +241,6 @@
     ids_came(1, *pair(3))
     for rel in pair(3):
         came(1, rel, 0)
-    ids_on((0, 3), 1, 1)
-    send_on((0, 3), 1, 1, 0)
     share_ids(*SLOTS[1:5])
     for rel in SLOTS[1:5]:
         share(rel, 0)
@@ -255,12 +255,11 @@
     for rel in pair(1):
         came(0, rel, 1)
     send_on((1, 0), 0, -1, 1)
-    for rel in pair(3):
-        came(1, rel, 1)
-    send_on((0, 1), 1, -1, 1)
     for rel in pair(1):
         for step in (1, -1):
             send_on(rel, 1, step, 1)
+    for rel in pair(3):
+        came(1, rel, 1)
     for rel in SLOTS[1:5]:
         share(rel, 1)
     arrived(("ru", 1), ("rd", 1))
@@ -270,61 +269,61 @@
     work(near, near_keys, far_keys)
     work(far, 0, far_keys)
 
-    arrived("mo", "ou", "od")
-    label_rows(0)
+    def others(k, count):
+        for row in (opp, near, far):
+            work(row, unit(k), unit(k + count))
+
     ids_came(0, (2, 0))
     for part in range(2):
         came(0, (2, 0), part)
     for step in (1, -1):
         ids_on((2, 0), 1, step)
         send_on((2, 0), 1, step)
+    ids_on((0, 3), 1, 1)
+    send_on((0, 3), 1, 1, 0)
+    send_on((0, 1), 1, -1, 1)
     share_ids((2, 0))
     share((2, 0))
+    arrived("mo", "ou", "od")
+    label_rows(0)
     work(opp, 0, far_keys)
+    beside(1)
+    work(own, near_keys, far_keys)
+    beside(3)
+    shared(*SLOTS[5:8])
+    others(5, 3)
+    beside(2)
+    shared(*pair(8))
+    others(8, 2)
     two_hops((0, 2))
-    work(own, near_keys, far_keys)
-    beside(1)
-
-    def others(k):
-        for row in (opp, near, far):
-            work(row, unit(k), unit(k + 2))
-
-    shared(*pair(5))
-    others(5)
-    beside(3)
-    shared(*pair(7))
-    others(7)
-    shared(*pair(9))
-    others(9)
-    beside(2)
-    work(own, unit(5), unit(9))
+    shared(*pair(10))
+    others(10, 2)
     two_hops((1, 2))
     two_hops((3, 2))
-    shared(*pair(11))
-    others(11)
+    shared(*pair(12))
+    work(opp, unit(12), unit(14))
     two_hops((2, 2))
-    shared(*pair(13))
-    work(opp, unit(13), unit(15))
+    shared((3, 2))
+    work(opp, unit(14), unit(15))
     shared((2, 2))
 
     work(opp, unit(15), unit(16))
     pass_on(0, OPP[0], 1)
     pass_on(1, OPP[1], -1)
-    work(near, unit(13), unit(16))
-    work(far, unit(13), unit(16))
+    work(near, unit(12), unit(16))
+    work(far, unit(12), unit(16))
     pass_on(2, UP[1], 1)
     pass_on(3, DOWN[0], -1)
-    work(own, unit(9), unit(13))
-    work(own, unit(13), unit(16))
+    work(own, unit(5), unit(11))
     take_in(0, UP[0])
     pass_on(4, UP[0], 1)
     take_in(1, DOWN[1])
     pass_on(5, DOWN[1], -1)
+    work(own, unit(11), unit(16))
     take_in(2, OWN[1])
     take_in(3, OWN[0])
-    take_in(4, OWN[0])
-    take_in(5, OWN[1])
-    out_ref[...] = acc[own:own + B, :]
+    out_ref[0:H, :] = acc[OWN[0]:OWN[0] + H, :] + decoded(4)
+    out_ref[H:B, :] = acc[OWN[1]:OWN[1] + H, :] + decoded(5)
     for copy in copies.values():
         copy.wait_send()
 

time: 70.8 us -> 69.6 us (0.983)
  Pallas kernels: 66.7 us -> 65.5 us
    pallas_call x1, Pallas kernels: 66.7 us -> 65.5 us  [local(): pl.pallas_call(kernel, out_shape=jax.ShapeDtypeStruct((B, D), jnp.float32...]
where the time goes in v4:
time: 69.6 us; the launch traced here: 69.4 us
  Pallas kernels  65.5 us (94%)
  local copies, waits for them, and re-layouts  1.67 us (2%)
  between operations  1.33 us (2%)
  other arithmetic  0.93 us (1%)
    pallas_call x1, Pallas kernels, local(): pl.pallas_call(kernel, out_shape=jax.ShapeDtypeStruct((B, D), jnp.float32...  65.5 us
    unnamed x6, local copies, waits for them, and re-layouts  1.67 us

profile of v4, /device:TPU:1, one launch (start us, length us, event | category | flops | bytes accessed | tf_op | source)
XLA Modules:
  0.0 69.4 jit_solution(5269992725930781026)
XLA Ops:
  1.3 0.0 copy-start.2
  1.3 0.0 copy-start.1
  1.3 0.7 copy-done.2
  2.0 0.0 copy-done.1
  2.0 0.0 copy-start
  2.0 1.0 %copy-done = bf16[256,768]{1,0:T(8,128)(2,1)S(1)} copy-done((bf16[256,768]{1,0:T(8,128)(2,1)S(1)}, bf16[256,768]{1,0:T(8,128)(2,1)}, u32[]{:S(2)}) %copy-start) | copy-done | bytes 393240
  3.0 65.5 %pair_gradients.1 = f32[256,768]{1,0:T(8,128)S(1)} custom-call(bf16[256,768]{1,0:T(8,128)(2,1)S(1)} %copy-done, s32[2,128]{1,0:T(2,128)S(1)} %bitcast.3, s32[2,128]{1,0:T(2,128)S(1)} %bitcast.4, f32[1]{0:T(128)S(6)} %copy.6.scale_ref, f32[1]{0:T(128)S(6)} %copy.7.bias_ref), custom_call_target="tpu_custom_call" | custom-call | tf_op jit(solution)/shard_map/pair_gradients/pallas_call | solution.py:336
  68.5 0.9 %broadcast_multiply_fusion = f32[256,768]{1,0:T(8,128)} fusion(f32[256,768]{1,0:T(8,128)S(1)} %pair_gradients.1, f32[]{:T(128)} %bitcast.2), kind=kLoop, calls=%fused_computation | loop fusion | flops 196608 | bytes 1572868 | tf_op jit(solution)/shard_map/mul | solution.py:364
Async XLA Ops:
  1.3 0.7 copy-start.2
  1.3 0.7 copy-start.1
  2.0 1.0 %copy-start = (bf16[256,768]{1,0:T(8,128)(2,1)S(1)}, bf16[256,768]{1,0:T(8,128)(2,1)}, u32[]{:S(2)}) copy-start(bf16[256,768]{1,0:T(8,128)(2,1)} %x_ref.1) | copy-start | bytes 1179652

commit v5 on v4

--- a/solution.py
+++ b/solution.py
@@ -178,18 +178,16 @@
         acc[at, :] += jnp.dot(slope, block, preferred_element_type=jnp.float32)
 
     def pass_on(piece, row, step):
-        sums = acc[pl.ds(row, H), :].reshape(H // 8, 8, D)
-        top = jnp.maximum(jnp.max(jnp.abs(sums), axis=0), 1e-30)
+        sums = acc[pl.ds(row, H), :]
+        top = jnp.maximum(jnp.max(jnp.abs(sums), axis=0, keepdims=True), 1e-30)
         coded_top[piece] = top
-        code = jnp.floor(sums * (32767.0 / top)[None] + 0.5).astype(jnp.int32)
-        coded[piece] = code.reshape(H, D).astype(jnp.int16)
+        coded[piece] = jnp.floor(sums * (32767.0 / top) + 0.5).astype(jnp.int32).astype(jnp.int16)
         start(("t", piece), coded_top.at[piece], landed_top.at[piece], line(step))
         start(("q", piece), coded.at[piece], landed.at[piece], line(step))
 
     def decoded(piece):
         arrived(("t", piece), ("q", piece))
-        sums = landed[piece].astype(jnp.int32).astype(jnp.float32).reshape(H // 8, 8, D)
-        return (sums * (landed_top[piece] * (1.0 / 32767.0))[None]).reshape(H, D)
+        return landed[piece].astype(jnp.int32).astype(jnp.float32) * (landed_top[piece] * (1.0 / 32767.0))
 
     def take_in(piece, row):
         acc[pl.ds(row, H), :] += decoded(piece)
@@ -349,9 +347,9 @@
             pltpu.VMEM((4 * B, H), jnp.int32),
             pltpu.VMEM((4 * B, H), jnp.int32),
             pltpu.VMEM((6, H, D), jnp.int16),
-            pltpu.VMEM((6, 8, D), jnp.float32),
+            pltpu.VMEM((6, 1, D), jnp.float32),
             pltpu.VMEM((6, H, D), jnp.int16),
-            pltpu.VMEM((6, 8, D), jnp.float32),
+            pltpu.VMEM((6, 1, D), jnp.float32),
             pltpu.SemaphoreType.DMA((3,)),
             pltpu.SemaphoreType.DMA((COPIES,)),
             pltpu.SemaphoreType.DMA((COPIES,)),

time: 69.6 us -> 68.3 us (0.981)
  Pallas kernels: 65.5 us -> 64.2 us
    pallas_call x1, Pallas kernels: 65.5 us -> 64.2 us  [local(): pl.pallas_call(kernel, out_shape=jax.ShapeDtypeStruct((B, D), jnp.float32...]
where the time goes in v5:
time: 68.3 us; the launch traced here: 68.1 us
  Pallas kernels  64.2 us (94%)
  local copies, waits for them, and re-layouts  1.67 us (2%)
  between operations  1.33 us (2%)
  other arithmetic  0.93 us (1%)
    pallas_call x1, Pallas kernels, local(): pl.pallas_call(kernel, out_shape=jax.ShapeDtypeStruct((B, D), jnp.float32...  64.2 us
    unnamed x6, local copies, waits for them, and re-layouts  1.67 us

profile of v5, /device:TPU:1, one launch (start us, length us, event | category | flops | bytes accessed | tf_op | source)
XLA Modules:
  0.0 68.1 jit_solution(3534049337552805137)
XLA Ops:
  1.3 0.0 copy-start.2
  1.3 0.0 copy-start.1
  1.3 0.7 copy-done.2
  2.0 0.0 copy-done.1
  2.0 0.0 copy-start
  2.0 1.0 %copy-done = bf16[256,768]{1,0:T(8,128)(2,1)S(1)} copy-done((bf16[256,768]{1,0:T(8,128)(2,1)S(1)}, bf16[256,768]{1,0:T(8,128)(2,1)}, u32[]{:S(2)}) %copy-start) | copy-done | bytes 393240
  3.0 64.2 %pair_gradients.1 = f32[256,768]{1,0:T(8,128)S(1)} custom-call(bf16[256,768]{1,0:T(8,128)(2,1)S(1)} %copy-done, s32[2,128]{1,0:T(2,128)S(1)} %bitcast.3, s32[2,128]{1,0:T(2,128)S(1)} %bitcast.4, f32[1]{0:T(128)S(6)} %copy.6.scale_ref, f32[1]{0:T(128)S(6)} %copy.7.bias_ref), custom_call_target="tpu_custom_call" | custom-call | tf_op jit(solution)/shard_map/pair_gradients/pallas_call | solution.py:334
  67.2 0.9 %broadcast_multiply_fusion = f32[256,768]{1,0:T(8,128)} fusion(f32[256,768]{1,0:T(8,128)S(1)} %pair_gradients.1, f32[]{:T(128)} %bitcast.2), kind=kLoop, calls=%fused_computation | loop fusion | flops 196608 | bytes 1572868 | tf_op jit(solution)/shard_map/mul | solution.py:362
Async XLA Ops:
  1.3 0.7 copy-start.2
  1.3 0.7 %copy-start.1 = (s32[256]{0:T(256)S(1)}, s32[256]{0:T(256)}, u32[]{:S(2)}) copy-start(s32[256]{0:T(256)} %param.6) | copy-start | bytes 3076
  2.0 1.0 %copy-start = (bf16[256,768]{1,0:T(8,128)(2,1)S(1)}, bf16[256,768]{1,0:T(8,128)(2,1)}, u32[]{:S(2)}) copy-start(bf16[256,768]{1,0:T(8,128)(2,1)} %x_ref.1) | copy-start | bytes 1179652

commit v6 on v5

--- a/solution.py
+++ b/solution.py
@@ -302,22 +302,26 @@
     work(opp, unit(12), unit(14))
     two_hops((2, 2))
     shared((3, 2))
-    work(opp, unit(14), unit(15))
+    for part in range(2):
+        key_ids[0:2, pl.ds(place(15, 0, part * H), H)] = key_meta[30, part]
+    work(opp, unit(14), unit(15) + B)
+    work(near, unit(12), unit(14))
     shared((2, 2))
 
-    work(opp, unit(15), unit(16))
+    work(opp, unit(15) + B, unit(16))
     pass_on(0, OPP[0], 1)
     pass_on(1, OPP[1], -1)
-    work(near, unit(12), unit(16))
+    work(near, unit(14), unit(16))
     work(far, unit(12), unit(16))
     pass_on(2, UP[1], 1)
     pass_on(3, DOWN[0], -1)
-    work(own, unit(5), unit(11))
+    work(own, unit(5), unit(9))
     take_in(0, UP[0])
     pass_on(4, UP[0], 1)
     take_in(1, DOWN[1])
     pass_on(5, DOWN[1], -1)
-    work(own, unit(11), unit(16))
+    work(own, unit(9), unit(12))
+    work(own, unit(12), unit(16))
     take_in(2, OWN[1])
     take_in(3, OWN[0])
     out_ref[0:H, :] = acc[OWN[0]:OWN[0] + H, :] + decoded(4)

time: 68.3 us -> 67.6 us (0.990)
  Pallas kernels: 64.2 us -> 63.5 us
    pallas_call x1, Pallas kernels: 64.2 us -> 63.5 us  [local(): pl.pallas_call(kernel, out_shape=jax.ShapeDtypeStruct((B, D), jnp.float32...]
where the time goes in v6:
time: 67.6 us; the launch traced here: 67.4 us
  Pallas kernels  63.5 us (94%)
  local copies, waits for them, and re-layouts  1.67 us (2%)
  between operations  1.33 us (2%)
  other arithmetic  0.93 us (1%)
    pallas_call x1, Pallas kernels, local(): pl.pallas_call(kernel, out_shape=jax.ShapeDtypeStruct((B, D), jnp.float32...  63.5 us
    unnamed x6, local copies, waits for them, and re-layouts  1.67 us

profile of v6, /device:TPU:1, one launch (start us, length us, event | category | flops | bytes accessed | tf_op | source)
XLA Modules:
  0.0 67.4 jit_solution(9386174614847255375)
XLA Ops:
  1.3 0.0 copy-start.2
  1.3 0.0 copy-start.1
  1.3 0.7 copy-done.2
  2.0 0.0 copy-done.1
  2.0 0.0 copy-start
  2.0 1.0 %copy-done = bf16[256,768]{1,0:T(8,128)(2,1)S(1)} copy-done((bf16[256,768]{1,0:T(8,128)(2,1)S(1)}, bf16[256,768]{1,0:T(8,128)(2,1)}, u32[]{:S(2)}) %copy-start) | copy-done | bytes 393240
  3.0 63.5 %pair_gradients.1 = f32[256,768]{1,0:T(8,128)S(1)} custom-call(bf16[256,768]{1,0:T(8,128)(2,1)S(1)} %copy-done, s32[2,128]{1,0:T(2,128)S(1)} %bitcast.3, s32[2,128]{1,0:T(2,128)S(1)} %bitcast.4, f32[1]{0:T(128)S(6)} %copy.6.scale_ref, f32[1]{0:T(128)S(6)} %copy.7.bias_ref), custom_call_target="tpu_custom_call" | custom-call | tf_op jit(solution)/shard_map/pair_gradients/pallas_call | solution.py:338
  66.5 0.9 %broadcast_multiply_fusion = f32[256,768]{1,0:T(8,128)} fusion(f32[256,768]{1,0:T(8,128)S(1)} %pair_gradients.1, f32[]{:T(128)} %bitcast.2), kind=kLoop, calls=%fused_computation | loop fusion | flops 196608 | bytes 1572868 | tf_op jit(solution)/shard_map/mul | solution.py:366
Async XLA Ops:
  1.3 0.7 %copy-start.2 = (s32[256]{0:T(256)S(1)}, s32[256]{0:T(256)}, u32[]{:S(2)}) copy-start(s32[256]{0:T(256)} %param.7) | copy-start | bytes 3076
  1.3 0.7 %copy-start.1 = (s32[256]{0:T(256)S(1)}, s32[256]{0:T(256)}, u32[]{:S(2)}) copy-start(s32[256]{0:T(256)} %param.6) | copy-start | bytes 3076
  2.0 1.0 %copy-start = (bf16[256,768]{1,0:T(8,128)(2,1)S(1)}, bf16[256,768]{1,0:T(8,128)(2,1)}, u32[]{:S(2)}) copy-start(bf16[256,768]{1,0:T(8,128)(2,1)} %x_ref.1) | copy-start | bytes 1179652

commit v7 on v6

--- a/solution.py
+++ b/solution.py
@@ -297,9 +297,11 @@
     shared(*pair(10))
     others(10, 2)
     two_hops((1, 2))
+    shared((0, 2))
+    work(opp, unit(12), unit(13))
     two_hops((3, 2))
-    shared(*pair(12))
-    work(opp, unit(12), unit(14))
+    shared((1, 2))
+    work(opp, unit(13), unit(14))
     two_hops((2, 2))
     shared((3, 2))
     for part in range(2):

time: 67.6 us -> 67.3 us (level)
  no operation moved by 1% of the time
where the time goes in v7:
time: 67.3 us; the launch traced here: 67.1 us
  Pallas kernels  63.1 us (94%)
  local copies, waits for them, and re-layouts  1.67 us (2%)
  between operations  1.33 us (2%)
  other arithmetic  0.93 us (1%)
    pallas_call x1, Pallas kernels, local(): pl.pallas_call(kernel, out_shape=jax.ShapeDtypeStruct((B, D), jnp.float32...  63.1 us
    unnamed x6, local copies, waits for them, and re-layouts  1.67 us

profile of v7, /device:TPU:1, one launch (start us, length us, event | category | flops | bytes accessed | tf_op | source)
XLA Modules:
  0.0 67.1 jit_solution(2258300745920598413)
XLA Ops:
  1.3 0.0 copy-start.2
  1.3 0.0 copy-start.1
  1.3 0.7 copy-done.2
  2.0 0.0 copy-done.1
  2.0 0.0 copy-start
  2.0 1.0 %copy-done = bf16[256,768]{1,0:T(8,128)(2,1)S(1)} copy-done((bf16[256,768]{1,0:T(8,128)(2,1)S(1)}, bf16[256,768]{1,0:T(8,128)(2,1)}, u32[]{:S(2)}) %copy-start) | copy-done | bytes 393240
  3.0 63.1 %pair_gradients.1 = f32[256,768]{1,0:T(8,128)S(1)} custom-call(bf16[256,768]{1,0:T(8,128)(2,1)S(1)} %copy-done, s32[2,128]{1,0:T(2,128)S(1)} %bitcast.3, s32[2,128]{1,0:T(2,128)S(1)} %bitcast.4, f32[1]{0:T(128)S(6)} %copy.6.scale_ref, f32[1]{0:T(128)S(6)} %copy.7.bias_ref), custom_call_target="tpu_custom_call" | custom-call | tf_op jit(solution)/shard_map/pair_gradients/pallas_call | solution.py:340
  66.2 0.9 %broadcast_multiply_fusion = f32[256,768]{1,0:T(8,128)} fusion(f32[256,768]{1,0:T(8,128)S(1)} %pair_gradients.1, f32[]{:T(128)} %bitcast.2), kind=kLoop, calls=%fused_computation | loop fusion | flops 196608 | bytes 1572868 | tf_op jit(solution)/shard_map/mul | solution.py:368
Async XLA Ops:
  1.3 0.7 %copy-start.2 = (s32[256]{0:T(256)S(1)}, s32[256]{0:T(256)}, u32[]{:S(2)}) copy-start(s32[256]{0:T(256)} %param.7) | copy-start | bytes 3076
  1.3 0.7 %copy-start.1 = (s32[256]{0:T(256)S(1)}, s32[256]{0:T(256)}, u32[]{:S(2)}) copy-start(s32[256]{0:T(256)} %param.6) | copy-start | bytes 3076
  2.0 1.0 %copy-start = (bf16[256,768]{1,0:T(8,128)(2,1)S(1)}, bf16[256,768]{1,0:T(8,128)(2,1)}, u32[]{:S(2)}) copy-start(bf16[256,768]{1,0:T(8,128)(2,1)} %x_ref.1) | copy-start | bytes 1179652
